TPU v7x, 128 devices: a whole 4x4x4 slice. The times are simulated.
128 devices in a mesh: site: 4 (over x), bond: 32 (over z, y, core).
Axes of the slice: x: 4, y: 4, z: 4, core: 2. Of those that a mesh axis runs over, the one named last changes fastest.
Arguments:
- start_rows: bfloat16 [1024, 4096], P(None, 'bond'), may hold values from -6 to 6
- site_tensors: bfloat16 [4, 4096, 8, 4096], P('site', None, None, 'bond'), may hold values from -0.09375 to 0.09375
- block_scales: float32 [4, 8, 32], P('site', None, 'bond'), may hold values from 0.25 to 1
- displacement: float32 [4, 8, 8], P('site'), may hold values from -0.9 to 0.9
- outcomes: int32 [4, 1024], P('site'), may hold values from 0 to 7
Outputs:
- leaving: bfloat16 [4, 1024, 4096], P('site', None, 'bond')
- log_norms: float32 [4, 1024], P('site')
Inputs may be any that keep to these rules, and one draw needn't show every extreme that they name: outcomes index the second dimension of displacement.
All inputs are finite; a program needn't handle non-finite values.
Results may differ from a plain program's by a relative error of at most 0.014.
Values may be sent and summed in bfloat16 or wider, within the bound.
No kernel may reach another device: no remote copies, remote signals or barrier semaphores. Data moves between devices by JAX's collectives and lax.ppermute only.
A program may use at most 64 MiB of HBM per device.

v0:
```python
import itertools

import jax
import jax.numpy as jnp
from jax import lax
from jax.experimental import pallas as pl
from jax.experimental.pallas import tpu as pltpu
from jax.sharding import Mesh, PartitionSpec as P

ROWS = 256
STRIDE = 256
NZ, NY, NC = 4, 4, 2
FIRST = (0, 1, 2, 3)
SECOND = (2, 1, 3)
BOND = ("z", "y", "core")
VMEM = pl.BlockSpec(memory_space=pltpu.VMEM)
HBM = pl.BlockSpec(memory_space=pltpu.HBM)


def fetch(parity, t_ref, held, sems):
    z, y = lax.axis_index("z"), lax.axis_index("y")
    for i, second in enumerate((0,) + SECOND):
        for k, first in enumerate(FIRST):
            back_z = (1 - parity) * second + parity * first
            back_y = (1 - parity) * first + parity * second
            block = lax.rem(z - back_z + NZ, NZ) * NY + lax.rem(y - back_y + NY, NY)
            j = i * NY + k
            pltpu.make_async_copy(t_ref.at[block, parity], held.at[j], sems.at[j]).start()


def turn(t_ref, out_ref, held, sems):
    blocks, size, _, cols = held.shape

    def step(j, carry):
        pltpu.make_async_copy(t_ref.at[0, 0], held.at[j], sems.at[j]).wait()
        bonds = pl.ds(pl.multiple_of(j * size, size), size)
        out_ref[:, bonds, pl.ds(0, cols)] = jnp.swapaxes(held[j], 0, 1)
        return carry

    lax.fori_loop(0, blocks, step, 0)


def give_kernel(t_ref, out_ref, held, sems):
    fetch(1 - lax.axis_index("core"), t_ref, held, sems)
    turn(t_ref, out_ref, held, sems)


def join_kernel(t_ref, got_ref, out_ref, held, sems, got_sem):
    cols = held.shape[3]
    fetch(lax.axis_index("core"), t_ref, held, sems)
    right = pltpu.make_async_copy(got_ref, out_ref.at[:, :, cols:], got_sem)
    right.start()
    turn(t_ref, out_ref, held, sems)
    right.wait()


def give(t):
    blocks, _, size, phys, cols = t.shape
    return pl.pallas_call(
        give_kernel,
        out_shape=jax.ShapeDtypeStruct((phys, blocks * size, cols), t.dtype),
        in_specs=[HBM],
        out_specs=VMEM,
        scratch_shapes=[
            pltpu.VMEM((blocks, size, phys, cols), t.dtype),
            pltpu.SemaphoreType.DMA((blocks,)),
        ],
        compiler_params=pltpu.CompilerParams(vmem_limit_bytes=56 * 2**20),
    )(t)


def join(t, got):
    blocks, _, size, phys, cols = t.shape
    return pl.pallas_call(
        join_kernel,
        out_shape=pltpu.VMEM((phys, blocks * size, 2 * cols), t.dtype),
        in_specs=[HBM, VMEM],
        out_specs=VMEM,
        scratch_shapes=[
            pltpu.VMEM((blocks, size, phys, cols), t.dtype),
            pltpu.SemaphoreType.DMA((blocks,)),
            pltpu.SemaphoreType.DMA,
        ],
        compiler_params=pltpu.CompilerParams(vmem_limit_bytes=40 * 2**20),
    )(t, got)


def contract_kernel(*refs):
    *x_refs, w_ref, own_ref, part_ref, mixed_in_ref, other_in_ref, mixed_ref, other_ref = refs
    add(x_refs, w_ref, own_ref, part_ref, mixed_in_ref[...], other_in_ref[...], mixed_ref, other_ref, True)


def open_kernel(*refs):
    *x_refs, w_ref, own_ref, part_ref, mixed_ref, other_ref = refs
    zeros = [jnp.zeros(ref.shape, jnp.float32) for ref in (mixed_ref, other_ref)]
    add(x_refs, w_ref, own_ref, part_ref, *zeros, mixed_ref, other_ref, False)


def add(x_refs, w_ref, own_ref, part_ref, mixed, other, mixed_ref, other_ref, last):
    cols = mixed_ref.shape[1]
    blocks = [ref[j] for ref in x_refs for j in range(NY)]
    rows = jnp.concatenate(blocks, axis=1)
    depth = rows.shape[1]
    bonds = pl.ds(w_ref.shape[1] - depth if last else 0, depth)
    other, squares = other[:, :cols], other[:, cols:]
    total = None
    for block in blocks:
        wide = block.astype(jnp.float32)
        total = wide * wide if total is None else total + wide * wide
    squares = squares + jnp.broadcast_to(jnp.sum(total, axis=1, keepdims=True), squares.shape)
    mixed_ref[...] = mixed
    other_ref[:, :cols] = other
    other_ref[:, cols:] = squares
    lane = lax.broadcasted_iota(jnp.int32, own_ref.shape, 1)

    def step(p, carry):
        prod = jnp.dot(rows, w_ref[p, bonds, :], preferred_element_type=jnp.float32)
        own, part = (
            jnp.sum(jnp.where(lane == p, ref[...], 0.0), axis=1, keepdims=True)
            for ref in (own_ref, part_ref)
        )
        mixed_ref[...] += own * prod[:, :cols]
        other_ref[:, :cols] += part * prod[:, cols:]
        return carry

    lax.fori_loop(0, w_ref.shape[0], step, 0, unroll=4)


def part_of(kernel, *operands):
    rows, cols = operands[0].shape[1:]
    return pl.pallas_call(
        kernel,
        out_shape=(
            jax.ShapeDtypeStruct((rows, cols), jnp.float32),
            jax.ShapeDtypeStruct((rows, 2 * cols), jnp.float32),
        ),
        in_specs=[VMEM] * len(operands),
        out_specs=(VMEM, VMEM),
        compiler_params=pltpu.CompilerParams(vmem_limit_bytes=16 * 2**20),
    )(*operands)


def contract(near, far, w, own, part):
    begun = part_of(open_kernel, near, far[0], w, own, part)
    return part_of(contract_kernel, *far[1:], w, own, part, *begun)


def local(start_rows, site_tensors, block_scales, displacement, outcomes):
    sites = lax.axis_size("site")
    chi, phys, cols = site_tensors.shape[1:]
    allrows = start_rows.shape[0]
    ngroups = -(-allrows // ROWS)
    bodies = ngroups + sites - 1
    position = lax.axis_index("site")
    devices = list(itertools.product(range(sites), range(NZ), range(NY), range(NC)))

    def index(site, z, y, core):
        return ((site % sites * NZ + z % NZ) * NY + y % NY) * NC + core

    def shifted(value, hop, first, second):
        pairs = []
        for site, z, y, core in devices:
            up, right = (second, first) if core == 0 else (first, second)
            pairs.append((index(site, z, y, core), index(site + hop, z + up, y + right, core)))
        return lax.ppermute(value, ("site",) + BOND, pairs)

    def to_partner(value):
        return lax.ppermute(value, "core", [(0, 1), (1, 0)])

    def ahead(value):
        return [shifted(value, 1, shift, 0) for shift in FIRST]

    def along_second(value):
        return [shifted(value, 0, 0, shift) for shift in SECOND]

    def start_piece(batch):
        first = min(batch, ngroups - 1) * STRIDE
        return start_rows[first : first + ROWS]

    tensor = site_tensors[0].reshape(NZ * NY, NC, cols, phys, cols)
    scale = block_scales[0][:, 0]
    partner_scale = to_partner(scale)
    onehot = (outcomes[0][:, None] == jnp.arange(phys, dtype=jnp.int32)[None, :]).astype(jnp.float32)
    weight = jnp.dot(onehot, displacement[0], precision=lax.Precision.HIGHEST)
    own_coef = weight * scale[None, :]
    part_coef = weight * partner_scale[None, :]
    def coefficients(body):
        first = jnp.clip(body - position, 0, ngroups - 1) * STRIDE
        return [lax.dynamic_slice_in_dim(c, first, ROWS, 0) for c in (own_coef, part_coef)]

    coefs = [coefficients(body) for body in range(bodies)]
    arriving = {0: ahead(start_piece(0))}
    sent = give(tensor)
    sent, coefs, closing, at_site = lax.optimization_barrier(
        (sent, coefs, position == sites - 1, [position == s for s in range(sites - 1)])
    )
    got = to_partner(sent)
    near = jnp.stack(arriving.pop(0))
    far = along_second(near)
    w = join(tensor, got)
    leaves, norms = [], []
    for body in range(bodies):
        more = body + 1 < bodies
        mixed, other = contract(near, far, w, *coefs[body])
        arrived = to_partner(other)
        norm = jnp.sqrt((other[:, cols:] + arrived[:, cols:]) / chi + 1e-06)
        leave = ((mixed + arrived[:, :cols]) / norm).astype(jnp.bfloat16)
        leaves.append(leave)
        norms.append(norm[:, 0])
        if more:
            arriving[body + 1] = ahead(jnp.where(closing, start_piece(body + 1), leave))
        if more:
            near = jnp.stack(arriving.pop(body + 1))
            far = along_second(near)
    leaves, norms = lax.optimization_barrier((leaves, norms))

    def placed(pieces):
        rows = []
        for b in range(ngroups):
            piece = pieces[b + sites - 1]
            for s in range(sites - 1):
                piece = jnp.where(at_site[s], pieces[b + s], piece)
            rows.append(piece if b + 1 == ngroups else piece[:STRIDE])
        return jnp.concatenate(rows, 0)

    return (placed(leaves)[None], jnp.log(placed(norms))[None])


def solution(mesh):
    fine = Mesh(mesh.devices.reshape(-1, NZ, NY, NC), ("site",) + BOND)
    return jax.shard_map(
        local,
        mesh=fine,
        in_specs=(
            P(None, BOND),
            P("site", None, None, BOND),
            P("site", None, BOND),
            P("site", None, None),
            P("site", None),
        ),
        out_specs=(P("site", None, BOND), P("site", None)),
        check_vma=False,
    )
```

profile of v0, /device:TPU:1, one launch (start us, length us, event | category | flops | bytes accessed | tf_op | source)
XLA Modules:
  0.0 192.8 jit_solution(16597349261539748786)
XLA Ops:
  2.2 4.4 %shard_map.68 = bf16[8,2048,128]{2,1,0:T(8,128)(2,1)} custom-call(bf16[16,2,128,8,128]{4,3,2,1,0:T(8,128)(2,1)} %bitcast.42), custom_call_target="tpu_custom_call" | custom-call | tf_op jit(solution)/shard_map/pallas_call | solution.py:59
  8.8 2.6 %collective-permute-start.2 = (bf16[256,128]{1,0:T(8,128)(2,1)S(1)}, bf16[256,128]{1,0:T(8,128)(2,1)S(1)}, u32[]{:S(2)}, u32[]{:S(2)}) collective-permute-start(bf16[256,128]{1,0:T(8,128)(2,1)S(1)} %slice.99), channel_id=1, source_target_pairs={{0,34},{1,41},{2,36},{3,43},{4,38},{5,45},{6,32},{7,47},{8,42},{9,... | collective-permute-start | bytes 196616 | tf_op jit(solution)/shard_map/ppermute | solution.py:165
  11.4 3.9 %collective-permute-start.3 = (bf16[256,128]{1,0:T(8,128)(2,1)S(1)}, bf16[256,128]{1,0:T(8,128)(2,1)S(1)}, u32[]{:S(2)}, u32[]{:S(2)}) collective-permute-start(bf16[256,128]{1,0:T(8,128)(2,1)S(1)} %slice.99), channel_id=1, source_target_pairs={{0,36},{1,49},{2,38},{3,51},{4,32},{5,53},{6,34},{7,55},{8,44},{9,... | collective-permute-start | bytes 196616 | tf_op jit(solution)/shard_map/ppermute | solution.py:165
  18.4 3.1 %collective-permute-done.4 = bf16[256,128]{1,0:T(8,128)(2,1)S(1)} collective-permute-done((bf16[256,128]{1,0:T(8,128)(2,1)S(1)}, bf16[256,128]{1,0:T(8,128)(2,1)S(1)}, u32[]{:S(2)}, u32[]{:S(2)}) %collective-permute-start.4) | collective-permute-done | bytes 65568 | tf_op jit(solution)/shard_map/ppermute | solution.py:165
  21.5 2.0 %collective-permute-start.8 = (bf16[4,256,128]{2,1,0:T(8,128)(2,1)S(1)}, bf16[4,256,128]{2,1,0:T(8,128)(2,1)S(1)}, u32[]{:S(2)}, u32[]{:S(2)}) collective-permute-start(bf16[4,256,128]{2,1,0:T(8,128)(2,1)S(1)} %pad_maximum_fusion.refs_0_), channel_id=1, source_target_pairs={{0,16},{1,5},{2,18},{3,7},{4,20},{5,1},{6,22},{7,3},{8,24},{9,13},... | collective-permute-start | bytes 786440 | tf_op jit(solution)/shard_map/ppermute | solution.py:165
  24.3 2.0 %collective-permute-start.6 = (bf16[4,256,128]{2,1,0:T(8,128)(2,1)S(1)}, bf16[4,256,128]{2,1,0:T(8,128)(2,1)S(1)}, u32[]{:S(2)}, u32[]{:S(2)}) collective-permute-start(bf16[4,256,128]{2,1,0:T(8,128)(2,1)S(1)} %pad_maximum_fusion.refs_0_), channel_id=1, source_target_pairs={{0,24},{1,7},{2,26},{3,1},{4,28},{5,3},{6,30},{7,5},{8,0},{9,15},{... | collective-permute-start | bytes 786440 | tf_op jit(solution)/shard_map/ppermute | solution.py:165
  26.2 2.4 %shard_map.69.refs_2_ = bf16[8,2048,256]{2,1,0:T(8,128)(2,1)S(1)} custom-call(bf16[16,2,128,8,128]{4,3,2,1,0:T(8,128)(2,1)} %bitcast.43, bf16[8,2048,128]{2,1,0:T(8,128)(2,1)S(1)} %collective-permute-done.7.got_ref), custom_call_target="tpu_custom_call" | custom-call | tf_op jit(solution)/shard_map/pallas_call | solution.py:74
  33.2 2.7 %collective-permute-start.9 = (f32[256,256]{1,0:T(8,128)S(1)}, f32[256,256]{1,0:T(8,128)S(1)}, u32[]{:S(2)}, u32[]{:S(2)}) collective-permute-start(f32[256,256]{1,0:T(8,128)S(1)} %get-tuple-element.70), channel_id=1, source_target_pairs={{0,1},{1,0},{2,3},{3,2},{4,5},{5,4},{6,7},{7,6},{8,9},{9,8},{10,11... | collective-permute-start | bytes 786440 | tf_op jit(solution)/shard_map/ppermute | solution.py:168
  37.7 2.3 %collective-permute-start.13 = (bf16[256,128]{1,0:T(8,128)(2,1)S(1)}, bf16[256,128]{1,0:T(8,128)(2,1)S(1)}, u32[]{:S(2)}, u32[]{:S(2)}) collective-permute-start(bf16[256,128]{1,0:T(8,128)(2,1)S(1)} %get-tuple-element.141), channel_id=1, source_target_pairs={{0,38},{1,57},{2,32},{3,59},{4,34},{5,61},{6,36},{7,63},{8,46},{9,... | collective-permute-start | bytes 196616 | tf_op jit(solution)/shard_map/ppermute | solution.py:165
  46.1 2.6 %collective-permute-done.11 = bf16[256,128]{1,0:T(8,128)(2,1)S(1)} collective-permute-done((bf16[256,128]{1,0:T(8,128)(2,1)S(1)}, bf16[256,128]{1,0:T(8,128)(2,1)S(1)}, u32[]{:S(2)}, u32[]{:S(2)}) %collective-permute-start.11) | collective-permute-done | bytes 65568 | tf_op jit(solution)/shard_map/ppermute | solution.py:165
  48.8 3.1 %collective-permute-start.14 = (bf16[4,256,128]{2,1,0:T(8,128)(2,1)S(1)}, bf16[4,256,128]{2,1,0:T(8,128)(2,1)S(1)}, u32[]{:S(2)}, u32[]{:S(2)}) collective-permute-start(bf16[4,256,128]{2,1,0:T(8,128)(2,1)S(1)} %pad_maximum_fusion.1.refs_0_), channel_id=1, source_target_pairs={{0,8},{1,3},{2,10},{3,5},{4,12},{5,7},{6,14},{7,1},{8,16},{9,11},{... | collective-permute-start | bytes 786440 | tf_op jit(solution)/shard_map/ppermute | solution.py:165
  51.9 4.0 %collective-permute-done.16.refs_1_ = bf16[4,256,128]{2,1,0:T(8,128)(2,1)S(1)} collective-permute-done((bf16[4,256,128]{2,1,0:T(8,128)(2,1)S(1)}, bf16[4,256,128]{2,1,0:T(8,128)(2,1)S(1)}, u32[]{:S(2)}, u32[]{:S(2)}) %collective-permute-start.16) | collective-permute-done | bytes 262176 | tf_op jit(solution)/shard_map/ppermute | solution.py:165
  64.9 2.4 %collective-permute-start.20 = (bf16[256,128]{1,0:T(8,128)(2,1)S(1)}, bf16[256,128]{1,0:T(8,128)(2,1)S(1)}, u32[]{:S(2)}, u32[]{:S(2)}) collective-permute-start(bf16[256,128]{1,0:T(8,128)(2,1)S(1)} %get-tuple-element.138), channel_id=1, source_target_pairs={{0,36},{1,49},{2,38},{3,51},{4,32},{5,53},{6,34},{7,55},{8,44},{9,... | collective-permute-start | bytes 196616 | tf_op jit(solution)/shard_map/ppermute | solution.py:165
  67.3 2.8 %collective-permute-start.21 = (bf16[256,128]{1,0:T(8,128)(2,1)S(1)}, bf16[256,128]{1,0:T(8,128)(2,1)S(1)}, u32[]{:S(2)}, u32[]{:S(2)}) collective-permute-start(bf16[256,128]{1,0:T(8,128)(2,1)S(1)} %get-tuple-element.138), channel_id=1, source_target_pairs={{0,38},{1,57},{2,32},{3,59},{4,34},{5,61},{6,36},{7,63},{8,46},{9,... | collective-permute-start | bytes 196616 | tf_op jit(solution)/shard_map/ppermute | solution.py:165
  74.7 2.2 %collective-permute-start.23 = (bf16[4,256,128]{2,1,0:T(8,128)(2,1)S(1)}, bf16[4,256,128]{2,1,0:T(8,128)(2,1)S(1)}, u32[]{:S(2)}, u32[]{:S(2)}) collective-permute-start(bf16[4,256,128]{2,1,0:T(8,128)(2,1)S(1)} %pad_maximum_fusion.2.refs_0_), channel_id=1, source_target_pairs={{0,24},{1,7},{2,26},{3,1},{4,28},{5,3},{6,30},{7,5},{8,0},{9,15},{... | collective-permute-start | bytes 786440 | tf_op jit(solution)/shard_map/ppermute | solution.py:165
  76.8 3.3 %collective-permute-done.24.refs_1_ = bf16[4,256,128]{2,1,0:T(8,128)(2,1)S(1)} collective-permute-done((bf16[4,256,128]{2,1,0:T(8,128)(2,1)S(1)}, bf16[4,256,128]{2,1,0:T(8,128)(2,1)S(1)}, u32[]{:S(2)}, u32[]{:S(2)}) %collective-permute-start.24) | collective-permute-done | bytes 262176 | tf_op jit(solution)/shard_map/ppermute | solution.py:165
  84.6 2.6 %collective-permute-start.25 = (f32[256,256]{1,0:T(8,128)S(1)}, f32[256,256]{1,0:T(8,128)S(1)}, u32[]{:S(2)}, u32[]{:S(2)}) collective-permute-start(f32[256,256]{1,0:T(8,128)S(1)} %get-tuple-element.83), channel_id=1, source_target_pairs={{0,1},{1,0},{2,3},{3,2},{4,5},{5,4},{6,7},{7,6},{8,9},{9,8},{10,11... | collective-permute-start | bytes 786440 | tf_op jit(solution)/shard_map/ppermute | solution.py:168
  89.8 3.2 %collective-permute-start.28 = (bf16[256,128]{1,0:T(8,128)(2,1)S(1)}, bf16[256,128]{1,0:T(8,128)(2,1)S(1)}, u32[]{:S(2)}, u32[]{:S(2)}) collective-permute-start(bf16[256,128]{1,0:T(8,128)(2,1)S(1)} %get-tuple-element.135), channel_id=1, source_target_pairs={{0,36},{1,49},{2,38},{3,51},{4,32},{5,53},{6,34},{7,55},{8,44},{9,... | collective-permute-start | bytes 196616 | tf_op jit(solution)/shard_map/ppermute | solution.py:165
  103.0 2.8 %collective-permute-done.32.refs_1_ = bf16[4,256,128]{2,1,0:T(8,128)(2,1)S(1)} collective-permute-done((bf16[4,256,128]{2,1,0:T(8,128)(2,1)S(1)}, bf16[4,256,128]{2,1,0:T(8,128)(2,1)S(1)}, u32[]{:S(2)}, u32[]{:S(2)}) %collective-permute-start.32) | collective-permute-done | bytes 262176 | tf_op jit(solution)/shard_map/ppermute | solution.py:165
  110.4 2.9 %collective-permute-start.33 = (f32[256,256]{1,0:T(8,128)S(1)}, f32[256,256]{1,0:T(8,128)S(1)}, u32[]{:S(2)}, u32[]{:S(2)}) collective-permute-start(f32[256,256]{1,0:T(8,128)S(1)} %get-tuple-element.89), channel_id=1, source_target_pairs={{0,1},{1,0},{2,3},{3,2},{4,5},{5,4},{6,7},{7,6},{8,9},{9,8},{10,11... | collective-permute-start | bytes 786440 | tf_op jit(solution)/shard_map/ppermute | solution.py:168
  116.2 3.2 %collective-permute-start.36 = (bf16[256,128]{1,0:T(8,128)(2,1)S(1)}, bf16[256,128]{1,0:T(8,128)(2,1)S(1)}, u32[]{:S(2)}, u32[]{:S(2)}) collective-permute-start(bf16[256,128]{1,0:T(8,128)(2,1)S(1)} %get-tuple-element.132), channel_id=1, source_target_pairs={{0,36},{1,49},{2,38},{3,51},{4,32},{5,53},{6,34},{7,55},{8,44},{9,... | collective-permute-start | bytes 196616 | tf_op jit(solution)/shard_map/ppermute | solution.py:165
  123.1 2.1 %collective-permute-done.37 = bf16[256,128]{1,0:T(8,128)(2,1)S(1)} collective-permute-done((bf16[256,128]{1,0:T(8,128)(2,1)S(1)}, bf16[256,128]{1,0:T(8,128)(2,1)S(1)}, u32[]{:S(2)}, u32[]{:S(2)}) %collective-permute-start.37) | collective-permute-done | bytes 65568 | tf_op jit(solution)/shard_map/ppermute | solution.py:165
  128.1 4.3 %collective-permute-done.40.refs_1_ = bf16[4,256,128]{2,1,0:T(8,128)(2,1)S(1)} collective-permute-done((bf16[4,256,128]{2,1,0:T(8,128)(2,1)S(1)}, bf16[4,256,128]{2,1,0:T(8,128)(2,1)S(1)}, u32[]{:S(2)}, u32[]{:S(2)}) %collective-permute-start.40) | collective-permute-done | bytes 262176 | tf_op jit(solution)/shard_map/ppermute | solution.py:165
  141.2 2.7 %collective-permute-start.44 = (bf16[256,128]{1,0:T(8,128)(2,1)S(1)}, bf16[256,128]{1,0:T(8,128)(2,1)S(1)}, u32[]{:S(2)}, u32[]{:S(2)}) collective-permute-start(bf16[256,128]{1,0:T(8,128)(2,1)S(1)} %get-tuple-element.129), channel_id=1, source_target_pairs={{0,36},{1,49},{2,38},{3,51},{4,32},{5,53},{6,34},{7,55},{8,44},{9,... | collective-permute-start | bytes 196616 | tf_op jit(solution)/shard_map/ppermute | solution.py:165
  143.9 2.1 %collective-permute-start.45 = (bf16[256,128]{1,0:T(8,128)(2,1)S(1)}, bf16[256,128]{1,0:T(8,128)(2,1)S(1)}, u32[]{:S(2)}, u32[]{:S(2)}) collective-permute-start(bf16[256,128]{1,0:T(8,128)(2,1)S(1)} %get-tuple-element.129), channel_id=1, source_target_pairs={{0,38},{1,57},{2,32},{3,59},{4,34},{5,61},{6,36},{7,63},{8,46},{9,... | collective-permute-start | bytes 196616 | tf_op jit(solution)/shard_map/ppermute | solution.py:165
  147.2 2.0 %collective-permute-done.44 = bf16[256,128]{1,0:T(8,128)(2,1)S(1)} collective-permute-done((bf16[256,128]{1,0:T(8,128)(2,1)S(1)}, bf16[256,128]{1,0:T(8,128)(2,1)S(1)}, u32[]{:S(2)}, u32[]{:S(2)}) %collective-permute-start.44) | collective-permute-done | bytes 65568 | tf_op jit(solution)/shard_map/ppermute | solution.py:165
  149.5 2.5 %collective-permute-start.48 = (bf16[4,256,128]{2,1,0:T(8,128)(2,1)S(1)}, bf16[4,256,128]{2,1,0:T(8,128)(2,1)S(1)}, u32[]{:S(2)}, u32[]{:S(2)}) collective-permute-start(bf16[4,256,128]{2,1,0:T(8,128)(2,1)S(1)} %pad_maximum_fusion.5.refs_0_), channel_id=1, source_target_pairs={{0,16},{1,5},{2,18},{3,7},{4,20},{5,1},{6,22},{7,3},{8,24},{9,13},... | collective-permute-start | bytes 786440 | tf_op jit(solution)/shard_map/ppermute | solution.py:165
  161.4 3.3 %collective-permute-start.49 = (f32[256,256]{1,0:T(8,128)S(1)}, f32[256,256]{1,0:T(8,128)S(1)}, u32[]{:S(2)}, u32[]{:S(2)}) collective-permute-start(f32[256,256]{1,0:T(8,128)S(1)} %get-tuple-element.101), channel_id=1, source_target_pairs={{0,1},{1,0},{2,3},{3,2},{4,5},{5,4},{6,7},{7,6},{8,9},{9,8},{10,11... | collective-permute-start | bytes 786440 | tf_op jit(solution)/shard_map/ppermute | solution.py:168
  167.2 2.9 %collective-permute-start.52 = (bf16[256,128]{1,0:T(8,128)(2,1)S(1)}, bf16[256,128]{1,0:T(8,128)(2,1)S(1)}, u32[]{:S(2)}, u32[]{:S(2)}) collective-permute-start(bf16[256,128]{1,0:T(8,128)(2,1)S(1)} %get-tuple-element.126), channel_id=1, source_target_pairs={{0,36},{1,49},{2,38},{3,51},{4,32},{5,53},{6,34},{7,55},{8,44},{9,... | collective-permute-start | bytes 196616 | tf_op jit(solution)/shard_map/ppermute | solution.py:165
  174.1 2.0 %collective-permute-done.53 = bf16[256,128]{1,0:T(8,128)(2,1)S(1)} collective-permute-done((bf16[256,128]{1,0:T(8,128)(2,1)S(1)}, bf16[256,128]{1,0:T(8,128)(2,1)S(1)}, u32[]{:S(2)}, u32[]{:S(2)}) %collective-permute-start.53) | collective-permute-done | bytes 65568 | tf_op jit(solution)/shard_map/ppermute | solution.py:165
  180.1 3.2 %collective-permute-done.56.refs_1_ = bf16[4,256,128]{2,1,0:T(8,128)(2,1)S(1)} collective-permute-done((bf16[4,256,128]{2,1,0:T(8,128)(2,1)S(1)}, bf16[4,256,128]{2,1,0:T(8,128)(2,1)S(1)}, u32[]{:S(2)}, u32[]{:S(2)}) %collective-permute-start.56) | collective-permute-done | bytes 262176 | tf_op jit(solution)/shard_map/ppermute | solution.py:165
  187.7 2.3 %collective-permute-start.57 = (f32[256,256]{1,0:T(8,128)S(1)}, f32[256,256]{1,0:T(8,128)S(1)}, u32[]{:S(2)}, u32[]{:S(2)}) collective-permute-start(f32[256,256]{1,0:T(8,128)S(1)} %get-tuple-element.107), channel_id=1, source_target_pairs={{0,1},{1,0},{2,3},{3,2},{4,5},{5,4},{6,7},{7,6},{8,9},{9,8},{10,11... | collective-permute-start | bytes 786440 | tf_op jit(solution)/shard_map/ppermute | solution.py:168
  (136 shorter events, 101.8 us)
Async XLA Ops:
  7.3 19.0 %collective-permute-start.7 = (bf16[8,2048,128]{2,1,0:T(8,128)(2,1)}, bf16[8,2048,128]{2,1,0:T(8,128)(2,1)S(1)}, u32[]{:S(2)}, u32[]{:S(2)}) collective-permute-start(bf16[8,2048,128]{2,1,0:T(8,128)(2,1)} %shard_map.68), channel_id=1, source_target_pairs={{0,1},{1,0},{2,3},{3,2},{4,5},{5,4},{6,7},{7,6},{8,9},{9,8},{10,11... | collective-permute-start | bytes 12582920 | tf_op jit(solution)/shard_map/ppermute | solution.py:168
  7.4 8.5 %collective-permute-start.1 = (bf16[256,128]{1,0:T(8,128)(2,1)S(1)}, bf16[256,128]{1,0:T(8,128)(2,1)S(1)}, u32[]{:S(2)}, u32[]{:S(2)}) collective-permute-start(bf16[256,128]{1,0:T(8,128)(2,1)S(1)} %slice.99), channel_id=1, source_target_pairs={{0,32},{1,33},{2,34},{3,35},{4,36},{5,37},{6,38},{7,39},{8,40},{9,... | collective-permute-start | bytes 196616 | tf_op jit(solution)/shard_map/ppermute | solution.py:165
  8.8 8.1 %collective-permute-start.2 = (bf16[256,128]{1,0:T(8,128)(2,1)S(1)}, bf16[256,128]{1,0:T(8,128)(2,1)S(1)}, u32[]{:S(2)}, u32[]{:S(2)}) collective-permute-start(bf16[256,128]{1,0:T(8,128)(2,1)S(1)} %slice.99), channel_id=1, source_target_pairs={{0,34},{1,41},{2,36},{3,43},{4,38},{5,45},{6,32},{7,47},{8,42},{9,... | collective-permute-start | bytes 196616 | tf_op jit(solution)/shard_map/ppermute | solution.py:165
  11.4 7.1 %collective-permute-start.3 = (bf16[256,128]{1,0:T(8,128)(2,1)S(1)}, bf16[256,128]{1,0:T(8,128)(2,1)S(1)}, u32[]{:S(2)}, u32[]{:S(2)}) collective-permute-start(bf16[256,128]{1,0:T(8,128)(2,1)S(1)} %slice.99), channel_id=1, source_target_pairs={{0,36},{1,49},{2,38},{3,51},{4,32},{5,53},{6,34},{7,55},{8,44},{9,... | collective-permute-start | bytes 196616 | tf_op jit(solution)/shard_map/ppermute | solution.py:165
  21.5 7.1 %collective-permute-start.8 = (bf16[4,256,128]{2,1,0:T(8,128)(2,1)S(1)}, bf16[4,256,128]{2,1,0:T(8,128)(2,1)S(1)}, u32[]{:S(2)}, u32[]{:S(2)}) collective-permute-start(bf16[4,256,128]{2,1,0:T(8,128)(2,1)S(1)} %pad_maximum_fusion.refs_0_), channel_id=1, source_target_pairs={{0,16},{1,5},{2,18},{3,7},{4,20},{5,1},{6,22},{7,3},{8,24},{9,13},... | collective-permute-start | bytes 786440 | tf_op jit(solution)/shard_map/ppermute | solution.py:165
  23.6 7.9 %collective-permute-start.5 = (bf16[4,256,128]{2,1,0:T(8,128)(2,1)S(1)}, bf16[4,256,128]{2,1,0:T(8,128)(2,1)S(1)}, u32[]{:S(2)}, u32[]{:S(2)}) collective-permute-start(bf16[4,256,128]{2,1,0:T(8,128)(2,1)S(1)} %pad_maximum_fusion.refs_0_), channel_id=1, source_target_pairs={{0,8},{1,3},{2,10},{3,5},{4,12},{5,7},{6,14},{7,1},{8,16},{9,11},{... | collective-permute-start | bytes 786440 | tf_op jit(solution)/shard_map/ppermute | solution.py:165
  24.3 7.2 %collective-permute-start.6 = (bf16[4,256,128]{2,1,0:T(8,128)(2,1)S(1)}, bf16[4,256,128]{2,1,0:T(8,128)(2,1)S(1)}, u32[]{:S(2)}, u32[]{:S(2)}) collective-permute-start(bf16[4,256,128]{2,1,0:T(8,128)(2,1)S(1)} %pad_maximum_fusion.refs_0_), channel_id=1, source_target_pairs={{0,24},{1,7},{2,26},{3,1},{4,28},{5,3},{6,30},{7,5},{8,0},{9,15},{... | collective-permute-start | bytes 786440 | tf_op jit(solution)/shard_map/ppermute | solution.py:165
  37.1 7.5 %collective-permute-start.12 = (bf16[256,128]{1,0:T(8,128)(2,1)S(1)}, bf16[256,128]{1,0:T(8,128)(2,1)S(1)}, u32[]{:S(2)}, u32[]{:S(2)}) collective-permute-start(bf16[256,128]{1,0:T(8,128)(2,1)S(1)} %get-tuple-element.141), channel_id=1, source_target_pairs={{0,36},{1,49},{2,38},{3,51},{4,32},{5,53},{6,34},{7,55},{8,44},{9,... | collective-permute-start | bytes 196616 | tf_op jit(solution)/shard_map/ppermute | solution.py:165
  37.7 7.8 %collective-permute-start.13 = (bf16[256,128]{1,0:T(8,128)(2,1)S(1)}, bf16[256,128]{1,0:T(8,128)(2,1)S(1)}, u32[]{:S(2)}, u32[]{:S(2)}) collective-permute-start(bf16[256,128]{1,0:T(8,128)(2,1)S(1)} %get-tuple-element.141), channel_id=1, source_target_pairs={{0,38},{1,57},{2,32},{3,59},{4,34},{5,61},{6,36},{7,63},{8,46},{9,... | collective-permute-start | bytes 196616 | tf_op jit(solution)/shard_map/ppermute | solution.py:165
  41.2 7.4 %collective-permute-start.11 = (bf16[256,128]{1,0:T(8,128)(2,1)S(1)}, bf16[256,128]{1,0:T(8,128)(2,1)S(1)}, u32[]{:S(2)}, u32[]{:S(2)}) collective-permute-start(bf16[256,128]{1,0:T(8,128)(2,1)S(1)} %get-tuple-element.141), channel_id=1, source_target_pairs={{0,34},{1,41},{2,36},{3,43},{4,38},{5,45},{6,32},{7,47},{8,42},{9,... | collective-permute-start | bytes 196616 | tf_op jit(solution)/shard_map/ppermute | solution.py:165
  48.7 7.1 %collective-permute-start.16 = (bf16[4,256,128]{2,1,0:T(8,128)(2,1)S(1)}, bf16[4,256,128]{2,1,0:T(8,128)(2,1)S(1)}, u32[]{:S(2)}, u32[]{:S(2)}) collective-permute-start(bf16[4,256,128]{2,1,0:T(8,128)(2,1)S(1)} %pad_maximum_fusion.1.refs_0_), channel_id=1, source_target_pairs={{0,16},{1,5},{2,18},{3,7},{4,20},{5,1},{6,22},{7,3},{8,24},{9,13},... | collective-permute-start | bytes 786440 | tf_op jit(solution)/shard_map/ppermute | solution.py:165
  48.8 9.6 %collective-permute-start.14 = (bf16[4,256,128]{2,1,0:T(8,128)(2,1)S(1)}, bf16[4,256,128]{2,1,0:T(8,128)(2,1)S(1)}, u32[]{:S(2)}, u32[]{:S(2)}) collective-permute-start(bf16[4,256,128]{2,1,0:T(8,128)(2,1)S(1)} %pad_maximum_fusion.1.refs_0_), channel_id=1, source_target_pairs={{0,8},{1,3},{2,10},{3,5},{4,12},{5,7},{6,14},{7,1},{8,16},{9,11},{... | collective-permute-start | bytes 786440 | tf_op jit(solution)/shard_map/ppermute | solution.py:165
  64.3 7.4 %collective-permute-start.19 = (bf16[256,128]{1,0:T(8,128)(2,1)S(1)}, bf16[256,128]{1,0:T(8,128)(2,1)S(1)}, u32[]{:S(2)}, u32[]{:S(2)}) collective-permute-start(bf16[256,128]{1,0:T(8,128)(2,1)S(1)} %get-tuple-element.138), channel_id=1, source_target_pairs={{0,34},{1,41},{2,36},{3,43},{4,38},{5,45},{6,32},{7,47},{8,42},{9,... | collective-permute-start | bytes 196616 | tf_op jit(solution)/shard_map/ppermute | solution.py:165
  64.9 8.1 %collective-permute-start.20 = (bf16[256,128]{1,0:T(8,128)(2,1)S(1)}, bf16[256,128]{1,0:T(8,128)(2,1)S(1)}, u32[]{:S(2)}, u32[]{:S(2)}) collective-permute-start(bf16[256,128]{1,0:T(8,128)(2,1)S(1)} %get-tuple-element.138), channel_id=1, source_target_pairs={{0,36},{1,49},{2,38},{3,51},{4,32},{5,53},{6,34},{7,55},{8,44},{9,... | collective-permute-start | bytes 196616 | tf_op jit(solution)/shard_map/ppermute | solution.py:165
  73.0 7.1 %collective-permute-start.24 = (bf16[4,256,128]{2,1,0:T(8,128)(2,1)S(1)}, bf16[4,256,128]{2,1,0:T(8,128)(2,1)S(1)}, u32[]{:S(2)}, u32[]{:S(2)}) collective-permute-start(bf16[4,256,128]{2,1,0:T(8,128)(2,1)S(1)} %pad_maximum_fusion.2.refs_0_), channel_id=1, source_target_pairs={{0,16},{1,5},{2,18},{3,7},{4,20},{5,1},{6,22},{7,3},{8,24},{9,13},... | collective-permute-start | bytes 786440 | tf_op jit(solution)/shard_map/ppermute | solution.py:165
  74.1 8.9 %collective-permute-start.22 = (bf16[4,256,128]{2,1,0:T(8,128)(2,1)S(1)}, bf16[4,256,128]{2,1,0:T(8,128)(2,1)S(1)}, u32[]{:S(2)}, u32[]{:S(2)}) collective-permute-start(bf16[4,256,128]{2,1,0:T(8,128)(2,1)S(1)} %pad_maximum_fusion.2.refs_0_), channel_id=1, source_target_pairs={{0,8},{1,3},{2,10},{3,5},{4,12},{5,7},{6,14},{7,1},{8,16},{9,11},{... | collective-permute-start | bytes 786440 | tf_op jit(solution)/shard_map/ppermute | solution.py:165
  74.7 8.3 %collective-permute-start.23 = (bf16[4,256,128]{2,1,0:T(8,128)(2,1)S(1)}, bf16[4,256,128]{2,1,0:T(8,128)(2,1)S(1)}, u32[]{:S(2)}, u32[]{:S(2)}) collective-permute-start(bf16[4,256,128]{2,1,0:T(8,128)(2,1)S(1)} %pad_maximum_fusion.2.refs_0_), channel_id=1, source_target_pairs={{0,24},{1,7},{2,26},{3,1},{4,28},{5,3},{6,30},{7,5},{8,0},{9,15},{... | collective-permute-start | bytes 786440 | tf_op jit(solution)/shard_map/ppermute | solution.py:165
  88.6 7.1 %collective-permute-start.27 = (bf16[256,128]{1,0:T(8,128)(2,1)S(1)}, bf16[256,128]{1,0:T(8,128)(2,1)S(1)}, u32[]{:S(2)}, u32[]{:S(2)}) collective-permute-start(bf16[256,128]{1,0:T(8,128)(2,1)S(1)} %get-tuple-element.135), channel_id=1, source_target_pairs={{0,34},{1,41},{2,36},{3,43},{4,38},{5,45},{6,32},{7,47},{8,42},{9,... | collective-permute-start | bytes 196616 | tf_op jit(solution)/shard_map/ppermute | solution.py:165
  89.8 7.3 %collective-permute-start.28 = (bf16[256,128]{1,0:T(8,128)(2,1)S(1)}, bf16[256,128]{1,0:T(8,128)(2,1)S(1)}, u32[]{:S(2)}, u32[]{:S(2)}) collective-permute-start(bf16[256,128]{1,0:T(8,128)(2,1)S(1)} %get-tuple-element.135), channel_id=1, source_target_pairs={{0,36},{1,49},{2,38},{3,51},{4,32},{5,53},{6,34},{7,55},{8,44},{9,... | collective-permute-start | bytes 196616 | tf_op jit(solution)/shard_map/ppermute | solution.py:165
  98.8 7.1 %collective-permute-start.32 = (bf16[4,256,128]{2,1,0:T(8,128)(2,1)S(1)}, bf16[4,256,128]{2,1,0:T(8,128)(2,1)S(1)}, u32[]{:S(2)}, u32[]{:S(2)}) collective-permute-start(bf16[4,256,128]{2,1,0:T(8,128)(2,1)S(1)} %pad_maximum_fusion.3.refs_0_), channel_id=1, source_target_pairs={{0,16},{1,5},{2,18},{3,7},{4,20},{5,1},{6,22},{7,3},{8,24},{9,13},... | collective-permute-start | bytes 786440 | tf_op jit(solution)/shard_map/ppermute | solution.py:165
  100.4 8.3 %collective-permute-start.30 = (bf16[4,256,128]{2,1,0:T(8,128)(2,1)S(1)}, bf16[4,256,128]{2,1,0:T(8,128)(2,1)S(1)}, u32[]{:S(2)}, u32[]{:S(2)}) collective-permute-start(bf16[4,256,128]{2,1,0:T(8,128)(2,1)S(1)} %pad_maximum_fusion.3.refs_0_), channel_id=1, source_target_pairs={{0,8},{1,3},{2,10},{3,5},{4,12},{5,7},{6,14},{7,1},{8,16},{9,11},{... | collective-permute-start | bytes 786440 | tf_op jit(solution)/shard_map/ppermute | solution.py:165
  101.4 7.3 %collective-permute-start.31 = (bf16[4,256,128]{2,1,0:T(8,128)(2,1)S(1)}, bf16[4,256,128]{2,1,0:T(8,128)(2,1)S(1)}, u32[]{:S(2)}, u32[]{:S(2)}) collective-permute-start(bf16[4,256,128]{2,1,0:T(8,128)(2,1)S(1)} %pad_maximum_fusion.3.refs_0_), channel_id=1, source_target_pairs={{0,24},{1,7},{2,26},{3,1},{4,28},{5,3},{6,30},{7,5},{8,0},{9,15},{... | collective-permute-start | bytes 786440 | tf_op jit(solution)/shard_map/ppermute | solution.py:165
  115.1 7.5 %collective-permute-start.35 = (bf16[256,128]{1,0:T(8,128)(2,1)S(1)}, bf16[256,128]{1,0:T(8,128)(2,1)S(1)}, u32[]{:S(2)}, u32[]{:S(2)}) collective-permute-start(bf16[256,128]{1,0:T(8,128)(2,1)S(1)} %get-tuple-element.132), channel_id=1, source_target_pairs={{0,34},{1,41},{2,36},{3,43},{4,38},{5,45},{6,32},{7,47},{8,42},{9,... | collective-permute-start | bytes 196616 | tf_op jit(solution)/shard_map/ppermute | solution.py:165
  125.2 7.1 %collective-permute-start.40 = (bf16[4,256,128]{2,1,0:T(8,128)(2,1)S(1)}, bf16[4,256,128]{2,1,0:T(8,128)(2,1)S(1)}, u32[]{:S(2)}, u32[]{:S(2)}) collective-permute-start(bf16[4,256,128]{2,1,0:T(8,128)(2,1)S(1)} %pad_maximum_fusion.4.refs_0_), channel_id=1, source_target_pairs={{0,16},{1,5},{2,18},{3,7},{4,20},{5,1},{6,22},{7,3},{8,24},{9,13},... | collective-permute-start | bytes 786440 | tf_op jit(solution)/shard_map/ppermute | solution.py:165
  125.4 9.5 %collective-permute-start.38 = (bf16[4,256,128]{2,1,0:T(8,128)(2,1)S(1)}, bf16[4,256,128]{2,1,0:T(8,128)(2,1)S(1)}, u32[]{:S(2)}, u32[]{:S(2)}) collective-permute-start(bf16[4,256,128]{2,1,0:T(8,128)(2,1)S(1)} %pad_maximum_fusion.4.refs_0_), channel_id=1, source_target_pairs={{0,8},{1,3},{2,10},{3,5},{4,12},{5,7},{6,14},{7,1},{8,16},{9,11},{... | collective-permute-start | bytes 786440 | tf_op jit(solution)/shard_map/ppermute | solution.py:165
  126.9 8.0 %collective-permute-start.39 = (bf16[4,256,128]{2,1,0:T(8,128)(2,1)S(1)}, bf16[4,256,128]{2,1,0:T(8,128)(2,1)S(1)}, u32[]{:S(2)}, u32[]{:S(2)}) collective-permute-start(bf16[4,256,128]{2,1,0:T(8,128)(2,1)S(1)} %pad_maximum_fusion.4.refs_0_), channel_id=1, source_target_pairs={{0,24},{1,7},{2,26},{3,1},{4,28},{5,3},{6,30},{7,5},{8,0},{9,15},{... | collective-permute-start | bytes 786440 | tf_op jit(solution)/shard_map/ppermute | solution.py:165
  141.2 8.0 %collective-permute-start.44 = (bf16[256,128]{1,0:T(8,128)(2,1)S(1)}, bf16[256,128]{1,0:T(8,128)(2,1)S(1)}, u32[]{:S(2)}, u32[]{:S(2)}) collective-permute-start(bf16[256,128]{1,0:T(8,128)(2,1)S(1)} %get-tuple-element.129), channel_id=1, source_target_pairs={{0,36},{1,49},{2,38},{3,51},{4,32},{5,53},{6,34},{7,55},{8,44},{9,... | collective-permute-start | bytes 196616 | tf_op jit(solution)/shard_map/ppermute | solution.py:165
  151.9 7.5 %collective-permute-start.46 = (bf16[4,256,128]{2,1,0:T(8,128)(2,1)S(1)}, bf16[4,256,128]{2,1,0:T(8,128)(2,1)S(1)}, u32[]{:S(2)}, u32[]{:S(2)}) collective-permute-start(bf16[4,256,128]{2,1,0:T(8,128)(2,1)S(1)} %pad_maximum_fusion.5.refs_0_), channel_id=1, source_target_pairs={{0,8},{1,3},{2,10},{3,5},{4,12},{5,7},{6,14},{7,1},{8,16},{9,11},{... | collective-permute-start | bytes 786440 | tf_op jit(solution)/shard_map/ppermute | solution.py:165
  166.2 7.4 %collective-permute-start.51 = (bf16[256,128]{1,0:T(8,128)(2,1)S(1)}, bf16[256,128]{1,0:T(8,128)(2,1)S(1)}, u32[]{:S(2)}, u32[]{:S(2)}) collective-permute-start(bf16[256,128]{1,0:T(8,128)(2,1)S(1)} %get-tuple-element.126), channel_id=1, source_target_pairs={{0,34},{1,41},{2,36},{3,43},{4,38},{5,45},{6,32},{7,47},{8,42},{9,... | collective-permute-start | bytes 196616 | tf_op jit(solution)/shard_map/ppermute | solution.py:165
  176.1 7.1 %collective-permute-start.56 = (bf16[4,256,128]{2,1,0:T(8,128)(2,1)S(1)}, bf16[4,256,128]{2,1,0:T(8,128)(2,1)S(1)}, u32[]{:S(2)}, u32[]{:S(2)}) collective-permute-start(bf16[4,256,128]{2,1,0:T(8,128)(2,1)S(1)} %pad_maximum_fusion.6.refs_0_), channel_id=1, source_target_pairs={{0,16},{1,5},{2,18},{3,7},{4,20},{5,1},{6,22},{7,3},{8,24},{9,13},... | collective-permute-start | bytes 786440 | tf_op jit(solution)/shard_map/ppermute | solution.py:165
  177.1 9.0 %collective-permute-start.54 = (bf16[4,256,128]{2,1,0:T(8,128)(2,1)S(1)}, bf16[4,256,128]{2,1,0:T(8,128)(2,1)S(1)}, u32[]{:S(2)}, u32[]{:S(2)}) collective-permute-start(bf16[4,256,128]{2,1,0:T(8,128)(2,1)S(1)} %pad_maximum_fusion.6.refs_0_), channel_id=1, source_target_pairs={{0,8},{1,3},{2,10},{3,5},{4,12},{5,7},{6,14},{7,1},{8,16},{9,11},{... | collective-permute-start | bytes 786440 | tf_op jit(solution)/shard_map/ppermute | solution.py:165
  178.5 7.6 %collective-permute-start.55 = (bf16[4,256,128]{2,1,0:T(8,128)(2,1)S(1)}, bf16[4,256,128]{2,1,0:T(8,128)(2,1)S(1)}, u32[]{:S(2)}, u32[]{:S(2)}) collective-permute-start(bf16[4,256,128]{2,1,0:T(8,128)(2,1)S(1)} %pad_maximum_fusion.6.refs_0_), channel_id=1, source_target_pairs={{0,24},{1,7},{2,26},{3,1},{4,28},{5,3},{6,30},{7,5},{8,0},{9,15},{... | collective-permute-start | bytes 786440 | tf_op jit(solution)/shard_map/ppermute | solution.py:165
  (30 other events, 167.8 us)
where the time goes:
time: 193 us
  starting transfers between devices  92.4 us (48%)
  waiting for transfers between devices  65.2 us (34%)
  Pallas kernels  30.5 us (16%)
  other arithmetic  2.2 us (1%)
    ppermute x49, starting transfers between devices, shifted(): return lax.ppermute(value, ('site',) + BOND, pairs)  73.7 us
    ppermute x49, waiting for transfers between devices, shifted(): return lax.ppermute(value, ('site',) + BOND, pairs)  57.4 us
    pallas_call x14, Pallas kernels, part_of(): pl.pallas_call(kernel, out_shape=(jax.ShapeDtypeStruct((rows, cols), jnp....  23.7 us
    ppermute x9, starting transfers between devices, to_partner(): return lax.ppermute(value, 'core', [(0, 1), (1, 0)])  18.8 us
    ppermute x9, waiting for transfers between devices, to_partner(): return lax.ppermute(value, 'core', [(0, 1), (1, 0)])  7.8 us
    pallas_call x1, Pallas kernels, give(): pl.pallas_call(give_kernel, out_shape=jax.ShapeDtypeStruct((phys, blocks...  4.42 us
  transfers between devices with their start and end apart: 58, of which 43 were waited for; matrix products, arithmetic and copies ran while one was open for 0% of the time, Pallas kernels for 10%

commit v1 on v0

--- a/solution.py
+++ b/solution.py
@@ -28,21 +28,34 @@
             pltpu.make_async_copy(t_ref.at[block, parity], held.at[j], sems.at[j]).start()
 
 
-def turn(t_ref, out_ref, held, sems):
+def turn(t_ref, out_ref, held, sems, then=lambda j: None):
     blocks, size, _, cols = held.shape
 
     def step(j, carry):
         pltpu.make_async_copy(t_ref.at[0, 0], held.at[j], sems.at[j]).wait()
         bonds = pl.ds(pl.multiple_of(j * size, size), size)
         out_ref[:, bonds, pl.ds(0, cols)] = jnp.swapaxes(held[j], 0, 1)
+        then(j)
         return carry
 
     lax.fori_loop(0, blocks, step, 0)
 
 
-def give_kernel(t_ref, out_ref, held, sems):
+def give_kernel(t_ref, out_ref, held, turned, sems, out_sems):
+    blocks, size = held.shape[:2]
     fetch(1 - lax.axis_index("core"), t_ref, held, sems)
-    turn(t_ref, out_ref, held, sems)
+
+    def store(j):
+        bonds = pl.ds(pl.multiple_of(j * size, size), size)
+        return pltpu.make_async_copy(turned.at[:, bonds, :], out_ref.at[:, bonds, :], out_sems.at[j])
+
+    turn(t_ref, turned, held, sems, lambda j: store(j).start())
+
+    def step(j, carry):
+        store(j).wait()
+        return carry
+
+    lax.fori_loop(0, blocks, step, 0)
 
 
 def join_kernel(t_ref, got_ref, out_ref, held, sems, got_sem):
@@ -60,9 +73,11 @@
         give_kernel,
         out_shape=jax.ShapeDtypeStruct((phys, blocks * size, cols), t.dtype),
         in_specs=[HBM],
-        out_specs=VMEM,
+        out_specs=HBM,
         scratch_shapes=[
             pltpu.VMEM((blocks, size, phys, cols), t.dtype),
+            pltpu.VMEM((phys, blocks * size, cols), t.dtype),
+            pltpu.SemaphoreType.DMA((blocks,)),
             pltpu.SemaphoreType.DMA((blocks,)),
         ],
         compiler_params=pltpu.CompilerParams(vmem_limit_bytes=56 * 2**20),
@@ -87,16 +102,16 @@
 
 def contract_kernel(*refs):
     *x_refs, w_ref, own_ref, part_ref, mixed_in_ref, other_in_ref, mixed_ref, other_ref = refs
-    add(x_refs, w_ref, own_ref, part_ref, mixed_in_ref[...], other_in_ref[...], mixed_ref, other_ref, True)
+    add(x_refs, w_ref, own_ref, part_ref, mixed_in_ref[...], other_in_ref[...], mixed_ref, other_ref, True, 8)
 
 
 def open_kernel(*refs):
     *x_refs, w_ref, own_ref, part_ref, mixed_ref, other_ref = refs
     zeros = [jnp.zeros(ref.shape, jnp.float32) for ref in (mixed_ref, other_ref)]
-    add(x_refs, w_ref, own_ref, part_ref, *zeros, mixed_ref, other_ref, False)
-
-
-def add(x_refs, w_ref, own_ref, part_ref, mixed, other, mixed_ref, other_ref, last):
+    add(x_refs, w_ref, own_ref, part_ref, *zeros, mixed_ref, other_ref, False, 1)
+
+
+def add(x_refs, w_ref, own_ref, part_ref, mixed, other, mixed_ref, other_ref, last, unroll):
     cols = mixed_ref.shape[1]
     blocks = [ref[j] for ref in x_refs for j in range(NY)]
     rows = jnp.concatenate(blocks, axis=1)
@@ -123,7 +138,7 @@
         other_ref[:, :cols] += part * prod[:, cols:]
         return carry
 
-    lax.fori_loop(0, w_ref.shape[0], step, 0, unroll=4)
+    lax.fori_loop(0, w_ref.shape[0], step, 0, unroll=unroll)
 
 
 def part_of(kernel, *operands):

time: 193 us -> 190 us (0.984)
  waiting for transfers between devices: 65.2 us -> 57.5 us
  Pallas kernels: 30.5 us -> 34.6 us
    ppermute x49, waiting for transfers between devices: 57.4 us -> 49.7 us  [shifted(): return lax.ppermute(value, ('site',) + BOND, pairs)]
    pallas_call x14, Pallas kernels: 23.7 us -> 28.4 us  [part_of(): pl.pallas_call(kernel, out_shape=(jax.ShapeDtypeStruct((rows, cols), jnp....]
  transfers between devices with their start and end apart: 58 -> 58, of which waited for: 43 -> 39; matrix products, arithmetic and copies ran while one was open for 0% -> 0% of each run, Pallas kernels for 10% -> 13%
where the time goes in v1:
time: 190 us
  starting transfers between devices  93 us (49%)
  waiting for transfers between devices  57.5 us (30%)
  Pallas kernels  34.6 us (18%)
  other arithmetic  2.2 us (1%)
    ppermute x49, starting transfers between devices, shifted(): return lax.ppermute(value, ('site',) + BOND, pairs)  73.4 us
    ppermute x49, waiting for transfers between devices, shifted(): return lax.ppermute(value, ('site',) + BOND, pairs)  49.7 us
    pallas_call x14, Pallas kernels, part_of(): pl.pallas_call(kernel, out_shape=(jax.ShapeDtypeStruct((rows, cols), jnp....  28.4 us
    ppermute x9, starting transfers between devices, to_partner(): return lax.ppermute(value, 'core', [(0, 1), (1, 0)])  19.6 us
    ppermute x9, waiting for transfers between devices, to_partner(): return lax.ppermute(value, 'core', [(0, 1), (1, 0)])  7.8 us
  transfers between devices with their start and end apart: 58, of which 39 were waited for; matrix products, arithmetic and copies ran while one was open for 0% of the time, Pallas kernels for 13%

profile of v1, /device:TPU:1, one launch (start us, length us, event | category | flops | bytes accessed | tf_op | source)
XLA Modules:
  0.0 189.8 jit_solution(9610201328460454245)
XLA Ops:
  2.2 3.8 %shard_map.68 = bf16[8,2048,128]{2,1,0:T(8,128)(2,1)} custom-call(bf16[16,2,128,8,128]{4,3,2,1,0:T(8,128)(2,1)} %bitcast.42), custom_call_target="tpu_custom_call" | custom-call | tf_op jit(solution)/shard_map/pallas_call | solution.py:72
  8.2 2.6 %collective-permute-start.2 = (bf16[256,128]{1,0:T(8,128)(2,1)S(1)}, bf16[256,128]{1,0:T(8,128)(2,1)S(1)}, u32[]{:S(2)}, u32[]{:S(2)}) collective-permute-start(bf16[256,128]{1,0:T(8,128)(2,1)S(1)} %slice.99), channel_id=1, source_target_pairs={{0,34},{1,41},{2,36},{3,43},{4,38},{5,45},{6,32},{7,47},{8,42},{9,... | collective-permute-start | bytes 196616 | tf_op jit(solution)/shard_map/ppermute | solution.py:180
  10.7 3.9 %collective-permute-start.3 = (bf16[256,128]{1,0:T(8,128)(2,1)S(1)}, bf16[256,128]{1,0:T(8,128)(2,1)S(1)}, u32[]{:S(2)}, u32[]{:S(2)}) collective-permute-start(bf16[256,128]{1,0:T(8,128)(2,1)S(1)} %slice.99), channel_id=1, source_target_pairs={{0,36},{1,49},{2,38},{3,51},{4,32},{5,53},{6,34},{7,55},{8,44},{9,... | collective-permute-start | bytes 196616 | tf_op jit(solution)/shard_map/ppermute | solution.py:180
  17.8 3.0 %collective-permute-done.4 = bf16[256,128]{1,0:T(8,128)(2,1)S(1)} collective-permute-done((bf16[256,128]{1,0:T(8,128)(2,1)S(1)}, bf16[256,128]{1,0:T(8,128)(2,1)S(1)}, u32[]{:S(2)}, u32[]{:S(2)}) %collective-permute-start.4) | collective-permute-done | bytes 65568 | tf_op jit(solution)/shard_map/ppermute | solution.py:180
  25.6 2.4 %shard_map.69.refs_2_ = bf16[8,2048,256]{2,1,0:T(8,128)(2,1)S(1)} custom-call(bf16[16,2,128,8,128]{4,3,2,1,0:T(8,128)(2,1)} %bitcast.43, bf16[8,2048,128]{2,1,0:T(8,128)(2,1)S(1)} %collective-permute-done.7.got_ref), custom_call_target="tpu_custom_call" | custom-call | tf_op jit(solution)/shard_map/pallas_call | solution.py:89
  28.1 2.7 %shard_map.70 = (f32[256,128]{1,0:T(8,128)S(1)}, f32[256,256]{1,0:T(8,128)S(1)}) custom-call(bf16[4,256,128]{2,1,0:T(8,128)(2,1)S(1)} %pad_maximum_fusion.refs_0_, bf16[4,256,128]{2,1,0:T(8,128)(2,1)S(1)} %collective-permute-done.8.refs_1_, bf16[8,2048,256]{2,1,0:T(8,128)(2,1)S(1)} %shard_map.69.refs_2_, f32[256,8]{1,0:T(8,128)S(1)} %get-tuple-element.65.refs_3_, ...), custom_call_target="tpu_custom_call" | custom-call | tf_op jit(solution)/shard_map/pallas_call | solution.py:146
  32.2 3.0 %collective-permute-start.9 = (f32[256,256]{1,0:T(8,128)S(1)}, f32[256,256]{1,0:T(8,128)S(1)}, u32[]{:S(2)}, u32[]{:S(2)}) collective-permute-start(f32[256,256]{1,0:T(8,128)S(1)} %get-tuple-element.70), channel_id=1, source_target_pairs={{0,1},{1,0},{2,3},{3,2},{4,5},{5,4},{6,7},{7,6},{8,9},{9,8},{10,11... | collective-permute-start | bytes 786440 | tf_op jit(solution)/shard_map/ppermute | solution.py:183
  40.3 2.4 %collective-permute-start.11 = (bf16[256,128]{1,0:T(8,128)(2,1)S(1)}, bf16[256,128]{1,0:T(8,128)(2,1)S(1)}, u32[]{:S(2)}, u32[]{:S(2)}) collective-permute-start(bf16[256,128]{1,0:T(8,128)(2,1)S(1)} %get-tuple-element.141), channel_id=1, source_target_pairs={{0,34},{1,41},{2,36},{3,43},{4,38},{5,45},{6,32},{7,47},{8,42},{9,... | collective-permute-start | bytes 196616 | tf_op jit(solution)/shard_map/ppermute | solution.py:180
  47.8 3.1 %collective-permute-start.14 = (bf16[4,256,128]{2,1,0:T(8,128)(2,1)S(1)}, bf16[4,256,128]{2,1,0:T(8,128)(2,1)S(1)}, u32[]{:S(2)}, u32[]{:S(2)}) collective-permute-start(bf16[4,256,128]{2,1,0:T(8,128)(2,1)S(1)} %pad_maximum_fusion.1.refs_0_), channel_id=1, source_target_pairs={{0,8},{1,3},{2,10},{3,5},{4,12},{5,7},{6,14},{7,1},{8,16},{9,11},{... | collective-permute-start | bytes 786440 | tf_op jit(solution)/shard_map/ppermute | solution.py:180
  50.9 4.0 %collective-permute-done.16.refs_1_ = bf16[4,256,128]{2,1,0:T(8,128)(2,1)S(1)} collective-permute-done((bf16[4,256,128]{2,1,0:T(8,128)(2,1)S(1)}, bf16[4,256,128]{2,1,0:T(8,128)(2,1)S(1)}, u32[]{:S(2)}, u32[]{:S(2)}) %collective-permute-start.16) | collective-permute-done | bytes 262176 | tf_op jit(solution)/shard_map/ppermute | solution.py:180
  54.9 2.7 %shard_map.72 = (f32[256,128]{1,0:T(8,128)S(1)}, f32[256,256]{1,0:T(8,128)S(1)}) custom-call(bf16[4,256,128]{2,1,0:T(8,128)(2,1)S(1)} %pad_maximum_fusion.1.refs_0_, bf16[4,256,128]{2,1,0:T(8,128)(2,1)S(1)} %collective-permute-done.16.refs_1_, bf16[8,2048,256]{2,1,0:T(8,128)(2,1)S(1)} %shard_map.69.refs_2_, f32[256,8]{1,0:T(8,128)S(1)} %get-tuple-element.72.refs_3_, ...), custom_call_target="tpu_custom_call" | custom-call | tf_op jit(solution)/shard_map/pallas_call | solution.py:146
  63.6 3.3 %collective-permute-start.20 = (bf16[256,128]{1,0:T(8,128)(2,1)S(1)}, bf16[256,128]{1,0:T(8,128)(2,1)S(1)}, u32[]{:S(2)}, u32[]{:S(2)}) collective-permute-start(bf16[256,128]{1,0:T(8,128)(2,1)S(1)} %get-tuple-element.138), channel_id=1, source_target_pairs={{0,36},{1,49},{2,38},{3,51},{4,32},{5,53},{6,34},{7,55},{8,44},{9,... | collective-permute-start | bytes 196616 | tf_op jit(solution)/shard_map/ppermute | solution.py:180
  66.9 2.5 %collective-permute-start.21 = (bf16[256,128]{1,0:T(8,128)(2,1)S(1)}, bf16[256,128]{1,0:T(8,128)(2,1)S(1)}, u32[]{:S(2)}, u32[]{:S(2)}) collective-permute-start(bf16[256,128]{1,0:T(8,128)(2,1)S(1)} %get-tuple-element.138), channel_id=1, source_target_pairs={{0,38},{1,57},{2,32},{3,59},{4,34},{5,61},{6,36},{7,63},{8,46},{9,... | collective-permute-start | bytes 196616 | tf_op jit(solution)/shard_map/ppermute | solution.py:180
  73.2 2.6 %collective-permute-start.23 = (bf16[4,256,128]{2,1,0:T(8,128)(2,1)S(1)}, bf16[4,256,128]{2,1,0:T(8,128)(2,1)S(1)}, u32[]{:S(2)}, u32[]{:S(2)}) collective-permute-start(bf16[4,256,128]{2,1,0:T(8,128)(2,1)S(1)} %pad_maximum_fusion.2.refs_0_), channel_id=1, source_target_pairs={{0,24},{1,7},{2,26},{3,1},{4,28},{5,3},{6,30},{7,5},{8,0},{9,15},{... | collective-permute-start | bytes 786440 | tf_op jit(solution)/shard_map/ppermute | solution.py:180
  75.8 4.3 %collective-permute-done.24.refs_1_ = bf16[4,256,128]{2,1,0:T(8,128)(2,1)S(1)} collective-permute-done((bf16[4,256,128]{2,1,0:T(8,128)(2,1)S(1)}, bf16[4,256,128]{2,1,0:T(8,128)(2,1)S(1)}, u32[]{:S(2)}, u32[]{:S(2)}) %collective-permute-start.24) | collective-permute-done | bytes 262176 | tf_op jit(solution)/shard_map/ppermute | solution.py:180
  80.1 2.7 %shard_map.74 = (f32[256,128]{1,0:T(8,128)S(1)}, f32[256,256]{1,0:T(8,128)S(1)}) custom-call(bf16[4,256,128]{2,1,0:T(8,128)(2,1)S(1)} %pad_maximum_fusion.2.refs_0_, bf16[4,256,128]{2,1,0:T(8,128)(2,1)S(1)} %collective-permute-done.24.refs_1_, bf16[8,2048,256]{2,1,0:T(8,128)(2,1)S(1)} %shard_map.69.refs_2_, f32[256,8]{1,0:T(8,128)S(1)} %get-tuple-element.78.refs_3_, ...), custom_call_target="tpu_custom_call" | custom-call | tf_op jit(solution)/shard_map/pallas_call | solution.py:146
  88.3 2.9 %collective-permute-start.28 = (bf16[256,128]{1,0:T(8,128)(2,1)S(1)}, bf16[256,128]{1,0:T(8,128)(2,1)S(1)}, u32[]{:S(2)}, u32[]{:S(2)}) collective-permute-start(bf16[256,128]{1,0:T(8,128)(2,1)S(1)} %get-tuple-element.135), channel_id=1, source_target_pairs={{0,36},{1,49},{2,38},{3,51},{4,32},{5,53},{6,34},{7,55},{8,44},{9,... | collective-permute-start | bytes 196616 | tf_op jit(solution)/shard_map/ppermute | solution.py:180
  101.4 2.5 %collective-permute-done.32.refs_1_ = bf16[4,256,128]{2,1,0:T(8,128)(2,1)S(1)} collective-permute-done((bf16[4,256,128]{2,1,0:T(8,128)(2,1)S(1)}, bf16[4,256,128]{2,1,0:T(8,128)(2,1)S(1)}, u32[]{:S(2)}, u32[]{:S(2)}) %collective-permute-start.32) | collective-permute-done | bytes 262176 | tf_op jit(solution)/shard_map/ppermute | solution.py:180
  104.0 2.7 %shard_map.76 = (f32[256,128]{1,0:T(8,128)S(1)}, f32[256,256]{1,0:T(8,128)S(1)}) custom-call(bf16[4,256,128]{2,1,0:T(8,128)(2,1)S(1)} %pad_maximum_fusion.3.refs_0_, bf16[4,256,128]{2,1,0:T(8,128)(2,1)S(1)} %collective-permute-done.32.refs_1_, bf16[8,2048,256]{2,1,0:T(8,128)(2,1)S(1)} %shard_map.69.refs_2_, f32[256,8]{1,0:T(8,128)S(1)} %get-tuple-element.84.refs_3_, ...), custom_call_target="tpu_custom_call" | custom-call | tf_op jit(solution)/shard_map/pallas_call | solution.py:146
  108.1 3.1 %collective-permute-start.33 = (f32[256,256]{1,0:T(8,128)S(1)}, f32[256,256]{1,0:T(8,128)S(1)}, u32[]{:S(2)}, u32[]{:S(2)}) collective-permute-start(f32[256,256]{1,0:T(8,128)S(1)} %get-tuple-element.89), channel_id=1, source_target_pairs={{0,1},{1,0},{2,3},{3,2},{4,5},{5,4},{6,7},{7,6},{8,9},{9,8},{10,11... | collective-permute-start | bytes 786440 | tf_op jit(solution)/shard_map/ppermute | solution.py:183
  114.4 2.9 %collective-permute-start.36 = (bf16[256,128]{1,0:T(8,128)(2,1)S(1)}, bf16[256,128]{1,0:T(8,128)(2,1)S(1)}, u32[]{:S(2)}, u32[]{:S(2)}) collective-permute-start(bf16[256,128]{1,0:T(8,128)(2,1)S(1)} %get-tuple-element.132), channel_id=1, source_target_pairs={{0,36},{1,49},{2,38},{3,51},{4,32},{5,53},{6,34},{7,55},{8,44},{9,... | collective-permute-start | bytes 196616 | tf_op jit(solution)/shard_map/ppermute | solution.py:180
  125.9 4.0 %collective-permute-done.40.refs_1_ = bf16[4,256,128]{2,1,0:T(8,128)(2,1)S(1)} collective-permute-done((bf16[4,256,128]{2,1,0:T(8,128)(2,1)S(1)}, bf16[4,256,128]{2,1,0:T(8,128)(2,1)S(1)}, u32[]{:S(2)}, u32[]{:S(2)}) %collective-permute-start.40) | collective-permute-done | bytes 262176 | tf_op jit(solution)/shard_map/ppermute | solution.py:180
  130.0 2.7 %shard_map.78 = (f32[256,128]{1,0:T(8,128)S(1)}, f32[256,256]{1,0:T(8,128)S(1)}) custom-call(bf16[4,256,128]{2,1,0:T(8,128)(2,1)S(1)} %pad_maximum_fusion.4.refs_0_, bf16[4,256,128]{2,1,0:T(8,128)(2,1)S(1)} %collective-permute-done.40.refs_1_, bf16[8,2048,256]{2,1,0:T(8,128)(2,1)S(1)} %shard_map.69.refs_2_, f32[256,8]{1,0:T(8,128)S(1)} %get-tuple-element.90.refs_3_, ...), custom_call_target="tpu_custom_call" | custom-call | tf_op jit(solution)/shard_map/pallas_call | solution.py:146
  134.1 2.4 %collective-permute-start.41 = (f32[256,256]{1,0:T(8,128)S(1)}, f32[256,256]{1,0:T(8,128)S(1)}, u32[]{:S(2)}, u32[]{:S(2)}) collective-permute-start(f32[256,256]{1,0:T(8,128)S(1)} %get-tuple-element.95), channel_id=1, source_target_pairs={{0,1},{1,0},{2,3},{3,2},{4,5},{5,4},{6,7},{7,6},{8,9},{9,8},{10,11... | collective-permute-start | bytes 786440 | tf_op jit(solution)/shard_map/ppermute | solution.py:183
  138.7 3.0 %collective-permute-start.44 = (bf16[256,128]{1,0:T(8,128)(2,1)S(1)}, bf16[256,128]{1,0:T(8,128)(2,1)S(1)}, u32[]{:S(2)}, u32[]{:S(2)}) collective-permute-start(bf16[256,128]{1,0:T(8,128)(2,1)S(1)} %get-tuple-element.129), channel_id=1, source_target_pairs={{0,36},{1,49},{2,38},{3,51},{4,32},{5,53},{6,34},{7,55},{8,44},{9,... | collective-permute-start | bytes 196616 | tf_op jit(solution)/shard_map/ppermute | solution.py:180
  151.5 2.8 %collective-permute-done.48.refs_1_ = bf16[4,256,128]{2,1,0:T(8,128)(2,1)S(1)} collective-permute-done((bf16[4,256,128]{2,1,0:T(8,128)(2,1)S(1)}, bf16[4,256,128]{2,1,0:T(8,128)(2,1)S(1)}, u32[]{:S(2)}, u32[]{:S(2)}) %collective-permute-start.48) | collective-permute-done | bytes 262176 | tf_op jit(solution)/shard_map/ppermute | solution.py:180
  154.4 2.7 %shard_map.80 = (f32[256,128]{1,0:T(8,128)S(1)}, f32[256,256]{1,0:T(8,128)S(1)}) custom-call(bf16[4,256,128]{2,1,0:T(8,128)(2,1)S(1)} %pad_maximum_fusion.5.refs_0_, bf16[4,256,128]{2,1,0:T(8,128)(2,1)S(1)} %collective-permute-done.48.refs_1_, bf16[8,2048,256]{2,1,0:T(8,128)(2,1)S(1)} %shard_map.69.refs_2_, f32[256,8]{1,0:T(8,128)S(1)} %get-tuple-element.96.refs_3_, ...), custom_call_target="tpu_custom_call" | custom-call | tf_op jit(solution)/shard_map/pallas_call | solution.py:146
  158.8 3.3 %collective-permute-start.49 = (f32[256,256]{1,0:T(8,128)S(1)}, f32[256,256]{1,0:T(8,128)S(1)}, u32[]{:S(2)}, u32[]{:S(2)}) collective-permute-start(f32[256,256]{1,0:T(8,128)S(1)} %get-tuple-element.101), channel_id=1, source_target_pairs={{0,1},{1,0},{2,3},{3,2},{4,5},{5,4},{6,7},{7,6},{8,9},{9,8},{10,11... | collective-permute-start | bytes 786440 | tf_op jit(solution)/shard_map/ppermute | solution.py:183
  164.4 2.9 %collective-permute-start.52 = (bf16[256,128]{1,0:T(8,128)(2,1)S(1)}, bf16[256,128]{1,0:T(8,128)(2,1)S(1)}, u32[]{:S(2)}, u32[]{:S(2)}) collective-permute-start(bf16[256,128]{1,0:T(8,128)(2,1)S(1)} %get-tuple-element.126), channel_id=1, source_target_pairs={{0,36},{1,49},{2,38},{3,51},{4,32},{5,53},{6,34},{7,55},{8,44},{9,... | collective-permute-start | bytes 196616 | tf_op jit(solution)/shard_map/ppermute | solution.py:180
  177.2 3.2 %collective-permute-done.56.refs_1_ = bf16[4,256,128]{2,1,0:T(8,128)(2,1)S(1)} collective-permute-done((bf16[4,256,128]{2,1,0:T(8,128)(2,1)S(1)}, bf16[4,256,128]{2,1,0:T(8,128)(2,1)S(1)}, u32[]{:S(2)}, u32[]{:S(2)}) %collective-permute-start.56) | collective-permute-done | bytes 262176 | tf_op jit(solution)/shard_map/ppermute | solution.py:180
  180.4 2.7 %shard_map.82 = (f32[256,128]{1,0:T(8,128)S(1)}, f32[256,256]{1,0:T(8,128)S(1)}) custom-call(bf16[4,256,128]{2,1,0:T(8,128)(2,1)S(1)} %pad_maximum_fusion.6.refs_0_, bf16[4,256,128]{2,1,0:T(8,128)(2,1)S(1)} %collective-permute-done.56.refs_1_, bf16[8,2048,256]{2,1,0:T(8,128)(2,1)S(1)} %shard_map.69.refs_2_, f32[256,8]{1,0:T(8,128)S(1)} %get-tuple-element.102.refs_3_, ...), custom_call_target="tpu_custom_call" | custom-call | tf_op jit(solution)/shard_map/pallas_call | solution.py:146
  184.5 2.5 %collective-permute-start.57 = (f32[256,256]{1,0:T(8,128)S(1)}, f32[256,256]{1,0:T(8,128)S(1)}, u32[]{:S(2)}, u32[]{:S(2)}) collective-permute-start(f32[256,256]{1,0:T(8,128)S(1)} %get-tuple-element.107), channel_id=1, source_target_pairs={{0,1},{1,0},{2,3},{3,2},{4,5},{5,4},{6,7},{7,6},{8,9},{9,8},{10,11... | collective-permute-start | bytes 786440 | tf_op jit(solution)/shard_map/ppermute | solution.py:183
  (136 shorter events, 93.2 us)
Async XLA Ops:
  6.6 19.0 %collective-permute-start.7 = (bf16[8,2048,128]{2,1,0:T(8,128)(2,1)}, bf16[8,2048,128]{2,1,0:T(8,128)(2,1)S(1)}, u32[]{:S(2)}, u32[]{:S(2)}) collective-permute-start(bf16[8,2048,128]{2,1,0:T(8,128)(2,1)} %shard_map.68), channel_id=1, source_target_pairs={{0,1},{1,0},{2,3},{3,2},{4,5},{5,4},{6,7},{7,6},{8,9},{9,8},{10,11... | collective-permute-start | bytes 12582920 | tf_op jit(solution)/shard_map/ppermute | solution.py:183
  6.8 8.5 %collective-permute-start.1 = (bf16[256,128]{1,0:T(8,128)(2,1)S(1)}, bf16[256,128]{1,0:T(8,128)(2,1)S(1)}, u32[]{:S(2)}, u32[]{:S(2)}) collective-permute-start(bf16[256,128]{1,0:T(8,128)(2,1)S(1)} %slice.99), channel_id=1, source_target_pairs={{0,32},{1,33},{2,34},{3,35},{4,36},{5,37},{6,38},{7,39},{8,40},{9,... | collective-permute-start | bytes 196616 | tf_op jit(solution)/shard_map/ppermute | solution.py:180
  8.2 8.1 %collective-permute-start.2 = (bf16[256,128]{1,0:T(8,128)(2,1)S(1)}, bf16[256,128]{1,0:T(8,128)(2,1)S(1)}, u32[]{:S(2)}, u32[]{:S(2)}) collective-permute-start(bf16[256,128]{1,0:T(8,128)(2,1)S(1)} %slice.99), channel_id=1, source_target_pairs={{0,34},{1,41},{2,36},{3,43},{4,38},{5,45},{6,32},{7,47},{8,42},{9,... | collective-permute-start | bytes 196616 | tf_op jit(solution)/shard_map/ppermute | solution.py:180
  10.7 7.1 %collective-permute-start.3 = (bf16[256,128]{1,0:T(8,128)(2,1)S(1)}, bf16[256,128]{1,0:T(8,128)(2,1)S(1)}, u32[]{:S(2)}, u32[]{:S(2)}) collective-permute-start(bf16[256,128]{1,0:T(8,128)(2,1)S(1)} %slice.99), channel_id=1, source_target_pairs={{0,36},{1,49},{2,38},{3,51},{4,32},{5,53},{6,34},{7,55},{8,44},{9,... | collective-permute-start | bytes 196616 | tf_op jit(solution)/shard_map/ppermute | solution.py:180
  20.9 7.1 %collective-permute-start.8 = (bf16[4,256,128]{2,1,0:T(8,128)(2,1)S(1)}, bf16[4,256,128]{2,1,0:T(8,128)(2,1)S(1)}, u32[]{:S(2)}, u32[]{:S(2)}) collective-permute-start(bf16[4,256,128]{2,1,0:T(8,128)(2,1)S(1)} %pad_maximum_fusion.refs_0_), channel_id=1, source_target_pairs={{0,16},{1,5},{2,18},{3,7},{4,20},{5,1},{6,22},{7,3},{8,24},{9,13},... | collective-permute-start | bytes 786440 | tf_op jit(solution)/shard_map/ppermute | solution.py:180
  22.9 7.9 %collective-permute-start.5 = (bf16[4,256,128]{2,1,0:T(8,128)(2,1)S(1)}, bf16[4,256,128]{2,1,0:T(8,128)(2,1)S(1)}, u32[]{:S(2)}, u32[]{:S(2)}) collective-permute-start(bf16[4,256,128]{2,1,0:T(8,128)(2,1)S(1)} %pad_maximum_fusion.refs_0_), channel_id=1, source_target_pairs={{0,8},{1,3},{2,10},{3,5},{4,12},{5,7},{6,14},{7,1},{8,16},{9,11},{... | collective-permute-start | bytes 786440 | tf_op jit(solution)/shard_map/ppermute | solution.py:180
  23.6 7.2 %collective-permute-start.6 = (bf16[4,256,128]{2,1,0:T(8,128)(2,1)S(1)}, bf16[4,256,128]{2,1,0:T(8,128)(2,1)S(1)}, u32[]{:S(2)}, u32[]{:S(2)}) collective-permute-start(bf16[4,256,128]{2,1,0:T(8,128)(2,1)S(1)} %pad_maximum_fusion.refs_0_), channel_id=1, source_target_pairs={{0,24},{1,7},{2,26},{3,1},{4,28},{5,3},{6,30},{7,5},{8,0},{9,15},{... | collective-permute-start | bytes 786440 | tf_op jit(solution)/shard_map/ppermute | solution.py:180
  36.4 7.4 %collective-permute-start.12 = (bf16[256,128]{1,0:T(8,128)(2,1)S(1)}, bf16[256,128]{1,0:T(8,128)(2,1)S(1)}, u32[]{:S(2)}, u32[]{:S(2)}) collective-permute-start(bf16[256,128]{1,0:T(8,128)(2,1)S(1)} %get-tuple-element.141), channel_id=1, source_target_pairs={{0,36},{1,49},{2,38},{3,51},{4,32},{5,53},{6,34},{7,55},{8,44},{9,... | collective-permute-start | bytes 196616 | tf_op jit(solution)/shard_map/ppermute | solution.py:180
  37.2 7.4 %collective-permute-start.13 = (bf16[256,128]{1,0:T(8,128)(2,1)S(1)}, bf16[256,128]{1,0:T(8,128)(2,1)S(1)}, u32[]{:S(2)}, u32[]{:S(2)}) collective-permute-start(bf16[256,128]{1,0:T(8,128)(2,1)S(1)} %get-tuple-element.141), channel_id=1, source_target_pairs={{0,38},{1,57},{2,32},{3,59},{4,34},{5,61},{6,36},{7,63},{8,46},{9,... | collective-permute-start | bytes 196616 | tf_op jit(solution)/shard_map/ppermute | solution.py:180
  40.3 7.4 %collective-permute-start.11 = (bf16[256,128]{1,0:T(8,128)(2,1)S(1)}, bf16[256,128]{1,0:T(8,128)(2,1)S(1)}, u32[]{:S(2)}, u32[]{:S(2)}) collective-permute-start(bf16[256,128]{1,0:T(8,128)(2,1)S(1)} %get-tuple-element.141), channel_id=1, source_target_pairs={{0,34},{1,41},{2,36},{3,43},{4,38},{5,45},{6,32},{7,47},{8,42},{9,... | collective-permute-start | bytes 196616 | tf_op jit(solution)/shard_map/ppermute | solution.py:180
  47.7 7.1 %collective-permute-start.16 = (bf16[4,256,128]{2,1,0:T(8,128)(2,1)S(1)}, bf16[4,256,128]{2,1,0:T(8,128)(2,1)S(1)}, u32[]{:S(2)}, u32[]{:S(2)}) collective-permute-start(bf16[4,256,128]{2,1,0:T(8,128)(2,1)S(1)} %pad_maximum_fusion.1.refs_0_), channel_id=1, source_target_pairs={{0,16},{1,5},{2,18},{3,7},{4,20},{5,1},{6,22},{7,3},{8,24},{9,13},... | collective-permute-start | bytes 786440 | tf_op jit(solution)/shard_map/ppermute | solution.py:180
  47.8 9.8 %collective-permute-start.14 = (bf16[4,256,128]{2,1,0:T(8,128)(2,1)S(1)}, bf16[4,256,128]{2,1,0:T(8,128)(2,1)S(1)}, u32[]{:S(2)}, u32[]{:S(2)}) collective-permute-start(bf16[4,256,128]{2,1,0:T(8,128)(2,1)S(1)} %pad_maximum_fusion.1.refs_0_), channel_id=1, source_target_pairs={{0,8},{1,3},{2,10},{3,5},{4,12},{5,7},{6,14},{7,1},{8,16},{9,11},{... | collective-permute-start | bytes 786440 | tf_op jit(solution)/shard_map/ppermute | solution.py:180
  63.0 7.4 %collective-permute-start.19 = (bf16[256,128]{1,0:T(8,128)(2,1)S(1)}, bf16[256,128]{1,0:T(8,128)(2,1)S(1)}, u32[]{:S(2)}, u32[]{:S(2)}) collective-permute-start(bf16[256,128]{1,0:T(8,128)(2,1)S(1)} %get-tuple-element.138), channel_id=1, source_target_pairs={{0,34},{1,41},{2,36},{3,43},{4,38},{5,45},{6,32},{7,47},{8,42},{9,... | collective-permute-start | bytes 196616 | tf_op jit(solution)/shard_map/ppermute | solution.py:180
  63.6 8.5 %collective-permute-start.20 = (bf16[256,128]{1,0:T(8,128)(2,1)S(1)}, bf16[256,128]{1,0:T(8,128)(2,1)S(1)}, u32[]{:S(2)}, u32[]{:S(2)}) collective-permute-start(bf16[256,128]{1,0:T(8,128)(2,1)S(1)} %get-tuple-element.138), channel_id=1, source_target_pairs={{0,36},{1,49},{2,38},{3,51},{4,32},{5,53},{6,34},{7,55},{8,44},{9,... | collective-permute-start | bytes 196616 | tf_op jit(solution)/shard_map/ppermute | solution.py:180
  72.9 7.1 %collective-permute-start.24 = (bf16[4,256,128]{2,1,0:T(8,128)(2,1)S(1)}, bf16[4,256,128]{2,1,0:T(8,128)(2,1)S(1)}, u32[]{:S(2)}, u32[]{:S(2)}) collective-permute-start(bf16[4,256,128]{2,1,0:T(8,128)(2,1)S(1)} %pad_maximum_fusion.2.refs_0_), channel_id=1, source_target_pairs={{0,16},{1,5},{2,18},{3,7},{4,20},{5,1},{6,22},{7,3},{8,24},{9,13},... | collective-permute-start | bytes 786440 | tf_op jit(solution)/shard_map/ppermute | solution.py:180
  73.0 9.8 %collective-permute-start.22 = (bf16[4,256,128]{2,1,0:T(8,128)(2,1)S(1)}, bf16[4,256,128]{2,1,0:T(8,128)(2,1)S(1)}, u32[]{:S(2)}, u32[]{:S(2)}) collective-permute-start(bf16[4,256,128]{2,1,0:T(8,128)(2,1)S(1)} %pad_maximum_fusion.2.refs_0_), channel_id=1, source_target_pairs={{0,8},{1,3},{2,10},{3,5},{4,12},{5,7},{6,14},{7,1},{8,16},{9,11},{... | collective-permute-start | bytes 786440 | tf_op jit(solution)/shard_map/ppermute | solution.py:180
  73.2 9.6 %collective-permute-start.23 = (bf16[4,256,128]{2,1,0:T(8,128)(2,1)S(1)}, bf16[4,256,128]{2,1,0:T(8,128)(2,1)S(1)}, u32[]{:S(2)}, u32[]{:S(2)}) collective-permute-start(bf16[4,256,128]{2,1,0:T(8,128)(2,1)S(1)} %pad_maximum_fusion.2.refs_0_), channel_id=1, source_target_pairs={{0,24},{1,7},{2,26},{3,1},{4,28},{5,3},{6,30},{7,5},{8,0},{9,15},{... | collective-permute-start | bytes 786440 | tf_op jit(solution)/shard_map/ppermute | solution.py:180
  87.0 7.1 %collective-permute-start.27 = (bf16[256,128]{1,0:T(8,128)(2,1)S(1)}, bf16[256,128]{1,0:T(8,128)(2,1)S(1)}, u32[]{:S(2)}, u32[]{:S(2)}) collective-permute-start(bf16[256,128]{1,0:T(8,128)(2,1)S(1)} %get-tuple-element.135), channel_id=1, source_target_pairs={{0,34},{1,41},{2,36},{3,43},{4,38},{5,45},{6,32},{7,47},{8,42},{9,... | collective-permute-start | bytes 196616 | tf_op jit(solution)/shard_map/ppermute | solution.py:180
  96.9 7.1 %collective-permute-start.32 = (bf16[4,256,128]{2,1,0:T(8,128)(2,1)S(1)}, bf16[4,256,128]{2,1,0:T(8,128)(2,1)S(1)}, u32[]{:S(2)}, u32[]{:S(2)}) collective-permute-start(bf16[4,256,128]{2,1,0:T(8,128)(2,1)S(1)} %pad_maximum_fusion.3.refs_0_), channel_id=1, source_target_pairs={{0,16},{1,5},{2,18},{3,7},{4,20},{5,1},{6,22},{7,3},{8,24},{9,13},... | collective-permute-start | bytes 786440 | tf_op jit(solution)/shard_map/ppermute | solution.py:180
  98.7 8.0 %collective-permute-start.30 = (bf16[4,256,128]{2,1,0:T(8,128)(2,1)S(1)}, bf16[4,256,128]{2,1,0:T(8,128)(2,1)S(1)}, u32[]{:S(2)}, u32[]{:S(2)}) collective-permute-start(bf16[4,256,128]{2,1,0:T(8,128)(2,1)S(1)} %pad_maximum_fusion.3.refs_0_), channel_id=1, source_target_pairs={{0,8},{1,3},{2,10},{3,5},{4,12},{5,7},{6,14},{7,1},{8,16},{9,11},{... | collective-permute-start | bytes 786440 | tf_op jit(solution)/shard_map/ppermute | solution.py:180
  113.2 7.4 %collective-permute-start.35 = (bf16[256,128]{1,0:T(8,128)(2,1)S(1)}, bf16[256,128]{1,0:T(8,128)(2,1)S(1)}, u32[]{:S(2)}, u32[]{:S(2)}) collective-permute-start(bf16[256,128]{1,0:T(8,128)(2,1)S(1)} %get-tuple-element.132), channel_id=1, source_target_pairs={{0,34},{1,41},{2,36},{3,43},{4,38},{5,45},{6,32},{7,47},{8,42},{9,... | collective-permute-start | bytes 196616 | tf_op jit(solution)/shard_map/ppermute | solution.py:180
  114.4 7.5 %collective-permute-start.36 = (bf16[256,128]{1,0:T(8,128)(2,1)S(1)}, bf16[256,128]{1,0:T(8,128)(2,1)S(1)}, u32[]{:S(2)}, u32[]{:S(2)}) collective-permute-start(bf16[256,128]{1,0:T(8,128)(2,1)S(1)} %get-tuple-element.132), channel_id=1, source_target_pairs={{0,36},{1,49},{2,38},{3,51},{4,32},{5,53},{6,34},{7,55},{8,44},{9,... | collective-permute-start | bytes 196616 | tf_op jit(solution)/shard_map/ppermute | solution.py:180
  122.8 7.1 %collective-permute-start.40 = (bf16[4,256,128]{2,1,0:T(8,128)(2,1)S(1)}, bf16[4,256,128]{2,1,0:T(8,128)(2,1)S(1)}, u32[]{:S(2)}, u32[]{:S(2)}) collective-permute-start(bf16[4,256,128]{2,1,0:T(8,128)(2,1)S(1)} %pad_maximum_fusion.4.refs_0_), channel_id=1, source_target_pairs={{0,16},{1,5},{2,18},{3,7},{4,20},{5,1},{6,22},{7,3},{8,24},{9,13},... | collective-permute-start | bytes 786440 | tf_op jit(solution)/shard_map/ppermute | solution.py:180
  123.3 9.5 %collective-permute-start.38 = (bf16[4,256,128]{2,1,0:T(8,128)(2,1)S(1)}, bf16[4,256,128]{2,1,0:T(8,128)(2,1)S(1)}, u32[]{:S(2)}, u32[]{:S(2)}) collective-permute-start(bf16[4,256,128]{2,1,0:T(8,128)(2,1)S(1)} %pad_maximum_fusion.4.refs_0_), channel_id=1, source_target_pairs={{0,8},{1,3},{2,10},{3,5},{4,12},{5,7},{6,14},{7,1},{8,16},{9,11},{... | collective-permute-start | bytes 786440 | tf_op jit(solution)/shard_map/ppermute | solution.py:180
  125.0 7.7 %collective-permute-start.39 = (bf16[4,256,128]{2,1,0:T(8,128)(2,1)S(1)}, bf16[4,256,128]{2,1,0:T(8,128)(2,1)S(1)}, u32[]{:S(2)}, u32[]{:S(2)}) collective-permute-start(bf16[4,256,128]{2,1,0:T(8,128)(2,1)S(1)} %pad_maximum_fusion.4.refs_0_), channel_id=1, source_target_pairs={{0,24},{1,7},{2,26},{3,1},{4,28},{5,3},{6,30},{7,5},{8,0},{9,15},{... | collective-permute-start | bytes 786440 | tf_op jit(solution)/shard_map/ppermute | solution.py:180
  138.7 8.3 %collective-permute-start.44 = (bf16[256,128]{1,0:T(8,128)(2,1)S(1)}, bf16[256,128]{1,0:T(8,128)(2,1)S(1)}, u32[]{:S(2)}, u32[]{:S(2)}) collective-permute-start(bf16[256,128]{1,0:T(8,128)(2,1)S(1)} %get-tuple-element.129), channel_id=1, source_target_pairs={{0,36},{1,49},{2,38},{3,51},{4,32},{5,53},{6,34},{7,55},{8,44},{9,... | collective-permute-start | bytes 196616 | tf_op jit(solution)/shard_map/ppermute | solution.py:180
  148.9 8.5 %collective-permute-start.46 = (bf16[4,256,128]{2,1,0:T(8,128)(2,1)S(1)}, bf16[4,256,128]{2,1,0:T(8,128)(2,1)S(1)}, u32[]{:S(2)}, u32[]{:S(2)}) collective-permute-start(bf16[4,256,128]{2,1,0:T(8,128)(2,1)S(1)} %pad_maximum_fusion.5.refs_0_), channel_id=1, source_target_pairs={{0,8},{1,3},{2,10},{3,5},{4,12},{5,7},{6,14},{7,1},{8,16},{9,11},{... | collective-permute-start | bytes 786440 | tf_op jit(solution)/shard_map/ppermute | solution.py:180
  163.8 7.3 %collective-permute-start.51 = (bf16[256,128]{1,0:T(8,128)(2,1)S(1)}, bf16[256,128]{1,0:T(8,128)(2,1)S(1)}, u32[]{:S(2)}, u32[]{:S(2)}) collective-permute-start(bf16[256,128]{1,0:T(8,128)(2,1)S(1)} %get-tuple-element.126), channel_id=1, source_target_pairs={{0,34},{1,41},{2,36},{3,43},{4,38},{5,45},{6,32},{7,47},{8,42},{9,... | collective-permute-start | bytes 196616 | tf_op jit(solution)/shard_map/ppermute | solution.py:180
  164.4 7.4 %collective-permute-start.52 = (bf16[256,128]{1,0:T(8,128)(2,1)S(1)}, bf16[256,128]{1,0:T(8,128)(2,1)S(1)}, u32[]{:S(2)}, u32[]{:S(2)}) collective-permute-start(bf16[256,128]{1,0:T(8,128)(2,1)S(1)} %get-tuple-element.126), channel_id=1, source_target_pairs={{0,36},{1,49},{2,38},{3,51},{4,32},{5,53},{6,34},{7,55},{8,44},{9,... | collective-permute-start | bytes 196616 | tf_op jit(solution)/shard_map/ppermute | solution.py:180
  173.3 7.1 %collective-permute-start.56 = (bf16[4,256,128]{2,1,0:T(8,128)(2,1)S(1)}, bf16[4,256,128]{2,1,0:T(8,128)(2,1)S(1)}, u32[]{:S(2)}, u32[]{:S(2)}) collective-permute-start(bf16[4,256,128]{2,1,0:T(8,128)(2,1)S(1)} %pad_maximum_fusion.6.refs_0_), channel_id=1, source_target_pairs={{0,16},{1,5},{2,18},{3,7},{4,20},{5,1},{6,22},{7,3},{8,24},{9,13},... | collective-permute-start | bytes 786440 | tf_op jit(solution)/shard_map/ppermute | solution.py:180
  174.2 8.9 %collective-permute-start.54 = (bf16[4,256,128]{2,1,0:T(8,128)(2,1)S(1)}, bf16[4,256,128]{2,1,0:T(8,128)(2,1)S(1)}, u32[]{:S(2)}, u32[]{:S(2)}) collective-permute-start(bf16[4,256,128]{2,1,0:T(8,128)(2,1)S(1)} %pad_maximum_fusion.6.refs_0_), channel_id=1, source_target_pairs={{0,8},{1,3},{2,10},{3,5},{4,12},{5,7},{6,14},{7,1},{8,16},{9,11},{... | collective-permute-start | bytes 786440 | tf_op jit(solution)/shard_map/ppermute | solution.py:180
  175.7 7.4 %collective-permute-start.55 = (bf16[4,256,128]{2,1,0:T(8,128)(2,1)S(1)}, bf16[4,256,128]{2,1,0:T(8,128)(2,1)S(1)}, u32[]{:S(2)}, u32[]{:S(2)}) collective-permute-start(bf16[4,256,128]{2,1,0:T(8,128)(2,1)S(1)} %pad_maximum_fusion.6.refs_0_), channel_id=1, source_target_pairs={{0,24},{1,7},{2,26},{3,1},{4,28},{5,3},{6,30},{7,5},{8,0},{9,15},{... | collective-permute-start | bytes 786440 | tf_op jit(solution)/shard_map/ppermute | solution.py:180
  (30 other events, 166.9 us)

commit v2 on v1

--- a/solution.py
+++ b/solution.py
@@ -7,8 +7,8 @@
 from jax.experimental.pallas import tpu as pltpu
 from jax.sharding import Mesh, PartitionSpec as P
 
-ROWS = 256
-STRIDE = 256
+ROWS = 352
+STRIDE = 336
 NZ, NY, NC = 4, 4, 2
 FIRST = (0, 1, 2, 3)
 SECOND = (2, 1, 3)
@@ -151,7 +151,7 @@
         ),
         in_specs=[VMEM] * len(operands),
         out_specs=(VMEM, VMEM),
-        compiler_params=pltpu.CompilerParams(vmem_limit_bytes=16 * 2**20),
+        compiler_params=pltpu.CompilerParams(vmem_limit_bytes=20 * 2**20),
     )(*operands)
 
 

time: 190 us -> 187 us (0.984)
  starting transfers between devices: 93 us -> 82.8 us
  waiting for transfers between devices: 57.5 us -> 64.1 us
    ppermute x49 -> x42, waiting for transfers between devices: 49.7 us -> 56.8 us  [shifted(): return lax.ppermute(value, ('site',) + BOND, pairs)]
    ppermute x49 -> x42, starting transfers between devices: 73.4 us -> 67.4 us  [shifted(): return lax.ppermute(value, ('site',) + BOND, pairs)]
    ppermute x9 -> x8, starting transfers between devices: 19.6 us -> 15.4 us  [to_partner(): return lax.ppermute(value, 'core', [(0, 1), (1, 0)])]
    ppermute x9 -> x8, waiting for transfers between devices: 7.8 us -> 7.23 us  [to_partner(): return lax.ppermute(value, 'core', [(0, 1), (1, 0)])]
    pallas_call x14 -> x12, Pallas kernels: 28.4 us -> 28.8 us  [part_of(): pl.pallas_call(kernel, out_shape=(jax.ShapeDtypeStruct((rows, cols), jnp....]
  transfers between devices with their start and end apart: 58 -> 50, of which waited for: 39 -> 39; matrix products, arithmetic and copies ran while one was open for 0% -> 0% of each run, Pallas kernels for 13% -> 13%
where the time goes in v2:
time: 187 us
  starting transfers between devices  82.8 us (44%)
  waiting for transfers between devices  64.1 us (34%)
  Pallas kernels  35 us (19%)
  other arithmetic  2.41 us (1%)
    ppermute x42, starting transfers between devices, shifted(): return lax.ppermute(value, ('site',) + BOND, pairs)  67.4 us
    ppermute x42, waiting for transfers between devices, shifted(): return lax.ppermute(value, ('site',) + BOND, pairs)  56.8 us
    pallas_call x12, Pallas kernels, part_of(): pl.pallas_call(kernel, out_shape=(jax.ShapeDtypeStruct((rows, cols), jnp....  28.8 us
    ppermute x8, starting transfers between devices, to_partner(): return lax.ppermute(value, 'core', [(0, 1), (1, 0)])  15.4 us
    ppermute x8, waiting for transfers between devices, to_partner(): return lax.ppermute(value, 'core', [(0, 1), (1, 0)])  7.23 us
    pallas_call x1, Pallas kernels, give(): pl.pallas_call(give_kernel, out_shape=jax.ShapeDtypeStruct((phys, blocks...  3.76 us
  transfers between devices with their start and end apart: 50, of which 39 were waited for; matrix products, arithmetic and copies ran while one was open for 0% of the time, Pallas kernels for 13%

profile of v2, /device:TPU:1, one launch (start us, length us, event | category | flops | bytes accessed | tf_op | source)
XLA Modules:
  0.0 186.9 jit_solution(3380324857367990751)
XLA Ops:
  2.2 3.8 %shard_map.68 = bf16[8,2048,128]{2,1,0:T(8,128)(2,1)} custom-call(bf16[16,2,128,8,128]{4,3,2,1,0:T(8,128)(2,1)} %bitcast.36), custom_call_target="tpu_custom_call" | custom-call | tf_op jit(solution)/shard_map/pallas_call | solution.py:72
  8.2 2.6 %collective-permute-start.2 = (bf16[352,128]{1,0:T(8,128)(2,1)S(1)}, bf16[352,128]{1,0:T(8,128)(2,1)S(1)}, u32[]{:S(2)}, u32[]{:S(2)}) collective-permute-start(bf16[352,128]{1,0:T(8,128)(2,1)S(1)} %slice.96), channel_id=1, source_target_pairs={{0,34},{1,41},{2,36},{3,43},{4,38},{5,45},{6,32},{7,47},{8,42},{9,... | collective-permute-start | bytes 270344 | tf_op jit(solution)/shard_map/ppermute | solution.py:180
  10.7 3.9 %collective-permute-start.3 = (bf16[352,128]{1,0:T(8,128)(2,1)S(1)}, bf16[352,128]{1,0:T(8,128)(2,1)S(1)}, u32[]{:S(2)}, u32[]{:S(2)}) collective-permute-start(bf16[352,128]{1,0:T(8,128)(2,1)S(1)} %slice.96), channel_id=1, source_target_pairs={{0,36},{1,49},{2,38},{3,51},{4,32},{5,53},{6,34},{7,55},{8,44},{9,... | collective-permute-start | bytes 270344 | tf_op jit(solution)/shard_map/ppermute | solution.py:180
  26.0 2.4 %shard_map.69.refs_2_ = bf16[8,2048,256]{2,1,0:T(8,128)(2,1)S(1)} custom-call(bf16[16,2,128,8,128]{4,3,2,1,0:T(8,128)(2,1)} %bitcast.37, bf16[8,2048,128]{2,1,0:T(8,128)(2,1)S(1)} %collective-permute-done.7.got_ref), custom_call_target="tpu_custom_call" | custom-call | tf_op jit(solution)/shard_map/pallas_call | solution.py:89
  29.6 3.1 %shard_map.70 = (f32[352,128]{1,0:T(8,128)S(1)}, f32[352,256]{1,0:T(8,128)S(1)}) custom-call(bf16[4,352,128]{2,1,0:T(8,128)(2,1)S(1)} %pad_maximum_fusion.refs_0_, bf16[4,352,128]{2,1,0:T(8,128)(2,1)S(1)} %collective-permute-done.8.refs_1_, bf16[8,2048,256]{2,1,0:T(8,128)(2,1)S(1)} %shard_map.69.refs_2_, f32[352,8]{1,0:T(8,128)S(1)} %get-tuple-element.57.refs_3_, ...), custom_call_target="tpu_custom_call" | custom-call | tf_op jit(solution)/shard_map/pallas_call | solution.py:146
  35.1 2.5 %collective-permute-start.9 = (f32[352,256]{1,0:T(8,128)S(1)}, f32[352,256]{1,0:T(8,128)S(1)}, u32[]{:S(2)}, u32[]{:S(2)}) collective-permute-start(f32[352,256]{1,0:T(8,128)S(1)} %get-tuple-element.62), channel_id=1, source_target_pairs={{0,1},{1,0},{2,3},{3,2},{4,5},{5,4},{6,7},{7,6},{8,9},{9,8},{10,11... | collective-permute-start | bytes 1081352 | tf_op jit(solution)/shard_map/ppermute | solution.py:183
  46.7 2.6 %collective-permute-done.13 = bf16[352,128]{1,0:T(8,128)(2,1)S(1)} collective-permute-done((bf16[352,128]{1,0:T(8,128)(2,1)S(1)}, bf16[352,128]{1,0:T(8,128)(2,1)S(1)}, u32[]{:S(2)}, u32[]{:S(2)}) %collective-permute-start.13) | collective-permute-done | bytes 90144 | tf_op jit(solution)/shard_map/ppermute | solution.py:180
  52.8 2.7 %collective-permute-start.14 = (bf16[4,352,128]{2,1,0:T(8,128)(2,1)S(1)}, bf16[4,352,128]{2,1,0:T(8,128)(2,1)S(1)}, u32[]{:S(2)}, u32[]{:S(2)}) collective-permute-start(bf16[4,352,128]{2,1,0:T(8,128)(2,1)S(1)} %pad_maximum_fusion.1.refs_0_), channel_id=1, source_target_pairs={{0,8},{1,3},{2,10},{3,5},{4,12},{5,7},{6,14},{7,1},{8,16},{9,11},{... | collective-permute-start | bytes 1081352 | tf_op jit(solution)/shard_map/ppermute | solution.py:180
  55.5 4.9 %collective-permute-done.16.refs_1_ = bf16[4,352,128]{2,1,0:T(8,128)(2,1)S(1)} collective-permute-done((bf16[4,352,128]{2,1,0:T(8,128)(2,1)S(1)}, bf16[4,352,128]{2,1,0:T(8,128)(2,1)S(1)}, u32[]{:S(2)}, u32[]{:S(2)}) %collective-permute-start.16) | collective-permute-done | bytes 360480 | tf_op jit(solution)/shard_map/ppermute | solution.py:180
  60.5 3.1 %shard_map.72 = (f32[352,128]{1,0:T(8,128)S(1)}, f32[352,256]{1,0:T(8,128)S(1)}) custom-call(bf16[4,352,128]{2,1,0:T(8,128)(2,1)S(1)} %pad_maximum_fusion.1.refs_0_, bf16[4,352,128]{2,1,0:T(8,128)(2,1)S(1)} %collective-permute-done.16.refs_1_, bf16[8,2048,256]{2,1,0:T(8,128)(2,1)S(1)} %shard_map.69.refs_2_, f32[352,8]{1,0:T(8,128)S(1)} %get-tuple-element.64.refs_3_, ...), custom_call_target="tpu_custom_call" | custom-call | tf_op jit(solution)/shard_map/pallas_call | solution.py:146
  70.3 2.7 %collective-permute-start.20 = (bf16[352,128]{1,0:T(8,128)(2,1)S(1)}, bf16[352,128]{1,0:T(8,128)(2,1)S(1)}, u32[]{:S(2)}, u32[]{:S(2)}) collective-permute-start(bf16[352,128]{1,0:T(8,128)(2,1)S(1)} %get-tuple-element.119), channel_id=1, source_target_pairs={{0,36},{1,49},{2,38},{3,51},{4,32},{5,53},{6,34},{7,55},{8,44},{9,... | collective-permute-start | bytes 270344 | tf_op jit(solution)/shard_map/ppermute | solution.py:180
  73.0 3.5 %collective-permute-start.21 = (bf16[352,128]{1,0:T(8,128)(2,1)S(1)}, bf16[352,128]{1,0:T(8,128)(2,1)S(1)}, u32[]{:S(2)}, u32[]{:S(2)}) collective-permute-start(bf16[352,128]{1,0:T(8,128)(2,1)S(1)} %get-tuple-element.119), channel_id=1, source_target_pairs={{0,38},{1,57},{2,32},{3,59},{4,34},{5,61},{6,36},{7,63},{8,46},{9,... | collective-permute-start | bytes 270344 | tf_op jit(solution)/shard_map/ppermute | solution.py:180
  82.6 2.7 %collective-permute-start.23 = (bf16[4,352,128]{2,1,0:T(8,128)(2,1)S(1)}, bf16[4,352,128]{2,1,0:T(8,128)(2,1)S(1)}, u32[]{:S(2)}, u32[]{:S(2)}) collective-permute-start(bf16[4,352,128]{2,1,0:T(8,128)(2,1)S(1)} %pad_maximum_fusion.2.refs_0_), channel_id=1, source_target_pairs={{0,24},{1,7},{2,26},{3,1},{4,28},{5,3},{6,30},{7,5},{8,0},{9,15},{... | collective-permute-start | bytes 1081352 | tf_op jit(solution)/shard_map/ppermute | solution.py:180
  85.3 4.2 %collective-permute-done.24.refs_1_ = bf16[4,352,128]{2,1,0:T(8,128)(2,1)S(1)} collective-permute-done((bf16[4,352,128]{2,1,0:T(8,128)(2,1)S(1)}, bf16[4,352,128]{2,1,0:T(8,128)(2,1)S(1)}, u32[]{:S(2)}, u32[]{:S(2)}) %collective-permute-start.24) | collective-permute-done | bytes 360480 | tf_op jit(solution)/shard_map/ppermute | solution.py:180
  89.5 3.1 %shard_map.74 = (f32[352,128]{1,0:T(8,128)S(1)}, f32[352,256]{1,0:T(8,128)S(1)}) custom-call(bf16[4,352,128]{2,1,0:T(8,128)(2,1)S(1)} %pad_maximum_fusion.2.refs_0_, bf16[4,352,128]{2,1,0:T(8,128)(2,1)S(1)} %collective-permute-done.24.refs_1_, bf16[8,2048,256]{2,1,0:T(8,128)(2,1)S(1)} %shard_map.69.refs_2_, f32[352,8]{1,0:T(8,128)S(1)} %get-tuple-element.70.refs_3_, ...), custom_call_target="tpu_custom_call" | custom-call | tf_op jit(solution)/shard_map/pallas_call | solution.py:146
  98.9 2.5 %collective-permute-start.28 = (bf16[352,128]{1,0:T(8,128)(2,1)S(1)}, bf16[352,128]{1,0:T(8,128)(2,1)S(1)}, u32[]{:S(2)}, u32[]{:S(2)}) collective-permute-start(bf16[352,128]{1,0:T(8,128)(2,1)S(1)} %get-tuple-element.116), channel_id=1, source_target_pairs={{0,36},{1,49},{2,38},{3,51},{4,32},{5,53},{6,34},{7,55},{8,44},{9,... | collective-permute-start | bytes 270344 | tf_op jit(solution)/shard_map/ppermute | solution.py:180
  101.4 2.7 %collective-permute-start.29 = (bf16[352,128]{1,0:T(8,128)(2,1)S(1)}, bf16[352,128]{1,0:T(8,128)(2,1)S(1)}, u32[]{:S(2)}, u32[]{:S(2)}) collective-permute-start(bf16[352,128]{1,0:T(8,128)(2,1)S(1)} %get-tuple-element.116), channel_id=1, source_target_pairs={{0,38},{1,57},{2,32},{3,59},{4,34},{5,61},{6,36},{7,63},{8,46},{9,... | collective-permute-start | bytes 270344 | tf_op jit(solution)/shard_map/ppermute | solution.py:180
  113.8 3.3 %collective-permute-done.32.refs_1_ = bf16[4,352,128]{2,1,0:T(8,128)(2,1)S(1)} collective-permute-done((bf16[4,352,128]{2,1,0:T(8,128)(2,1)S(1)}, bf16[4,352,128]{2,1,0:T(8,128)(2,1)S(1)}, u32[]{:S(2)}, u32[]{:S(2)}) %collective-permute-start.32) | collective-permute-done | bytes 360480 | tf_op jit(solution)/shard_map/ppermute | solution.py:180
  117.1 3.1 %shard_map.76 = (f32[352,128]{1,0:T(8,128)S(1)}, f32[352,256]{1,0:T(8,128)S(1)}) custom-call(bf16[4,352,128]{2,1,0:T(8,128)(2,1)S(1)} %pad_maximum_fusion.3.refs_0_, bf16[4,352,128]{2,1,0:T(8,128)(2,1)S(1)} %collective-permute-done.32.refs_1_, bf16[8,2048,256]{2,1,0:T(8,128)(2,1)S(1)} %shard_map.69.refs_2_, f32[352,8]{1,0:T(8,128)S(1)} %get-tuple-element.76.refs_3_, ...), custom_call_target="tpu_custom_call" | custom-call | tf_op jit(solution)/shard_map/pallas_call | solution.py:146
  128.1 2.5 %collective-permute-start.36 = (bf16[352,128]{1,0:T(8,128)(2,1)S(1)}, bf16[352,128]{1,0:T(8,128)(2,1)S(1)}, u32[]{:S(2)}, u32[]{:S(2)}) collective-permute-start(bf16[352,128]{1,0:T(8,128)(2,1)S(1)} %get-tuple-element.113), channel_id=1, source_target_pairs={{0,36},{1,49},{2,38},{3,51},{4,32},{5,53},{6,34},{7,55},{8,44},{9,... | collective-permute-start | bytes 270344 | tf_op jit(solution)/shard_map/ppermute | solution.py:180
  130.6 2.5 %collective-permute-start.37 = (bf16[352,128]{1,0:T(8,128)(2,1)S(1)}, bf16[352,128]{1,0:T(8,128)(2,1)S(1)}, u32[]{:S(2)}, u32[]{:S(2)}) collective-permute-start(bf16[352,128]{1,0:T(8,128)(2,1)S(1)} %get-tuple-element.113), channel_id=1, source_target_pairs={{0,38},{1,57},{2,32},{3,59},{4,34},{5,61},{6,36},{7,63},{8,46},{9,... | collective-permute-start | bytes 270344 | tf_op jit(solution)/shard_map/ppermute | solution.py:180
  133.1 2.5 %collective-permute-done.35 = bf16[352,128]{1,0:T(8,128)(2,1)S(1)} collective-permute-done((bf16[352,128]{1,0:T(8,128)(2,1)S(1)}, bf16[352,128]{1,0:T(8,128)(2,1)S(1)}, u32[]{:S(2)}, u32[]{:S(2)}) %collective-permute-start.35) | collective-permute-done | bytes 90144 | tf_op jit(solution)/shard_map/ppermute | solution.py:180
  137.3 3.7 %collective-permute-start.40 = (bf16[4,352,128]{2,1,0:T(8,128)(2,1)S(1)}, bf16[4,352,128]{2,1,0:T(8,128)(2,1)S(1)}, u32[]{:S(2)}, u32[]{:S(2)}) collective-permute-start(bf16[4,352,128]{2,1,0:T(8,128)(2,1)S(1)} %pad_maximum_fusion.4.refs_0_), channel_id=1, source_target_pairs={{0,16},{1,5},{2,18},{3,7},{4,20},{5,1},{6,22},{7,3},{8,24},{9,13},... | collective-permute-start | bytes 1081352 | tf_op jit(solution)/shard_map/ppermute | solution.py:180
  141.1 2.7 %collective-permute-start.39 = (bf16[4,352,128]{2,1,0:T(8,128)(2,1)S(1)}, bf16[4,352,128]{2,1,0:T(8,128)(2,1)S(1)}, u32[]{:S(2)}, u32[]{:S(2)}) collective-permute-start(bf16[4,352,128]{2,1,0:T(8,128)(2,1)S(1)} %pad_maximum_fusion.4.refs_0_), channel_id=1, source_target_pairs={{0,24},{1,7},{2,26},{3,1},{4,28},{5,3},{6,30},{7,5},{8,0},{9,15},{... | collective-permute-start | bytes 1081352 | tf_op jit(solution)/shard_map/ppermute | solution.py:180
  143.8 2.4 %collective-permute-done.40.refs_1_ = bf16[4,352,128]{2,1,0:T(8,128)(2,1)S(1)} collective-permute-done((bf16[4,352,128]{2,1,0:T(8,128)(2,1)S(1)}, bf16[4,352,128]{2,1,0:T(8,128)(2,1)S(1)}, u32[]{:S(2)}, u32[]{:S(2)}) %collective-permute-start.40) | collective-permute-done | bytes 360480 | tf_op jit(solution)/shard_map/ppermute | solution.py:180
  146.2 3.1 %shard_map.78 = (f32[352,128]{1,0:T(8,128)S(1)}, f32[352,256]{1,0:T(8,128)S(1)}) custom-call(bf16[4,352,128]{2,1,0:T(8,128)(2,1)S(1)} %pad_maximum_fusion.4.refs_0_, bf16[4,352,128]{2,1,0:T(8,128)(2,1)S(1)} %collective-permute-done.40.refs_1_, bf16[8,2048,256]{2,1,0:T(8,128)(2,1)S(1)} %shard_map.69.refs_2_, f32[352,8]{1,0:T(8,128)S(1)} %get-tuple-element.82.refs_3_, ...), custom_call_target="tpu_custom_call" | custom-call | tf_op jit(solution)/shard_map/pallas_call | solution.py:146
  151.7 3.3 %collective-permute-start.41 = (f32[352,256]{1,0:T(8,128)S(1)}, f32[352,256]{1,0:T(8,128)S(1)}, u32[]{:S(2)}, u32[]{:S(2)}) collective-permute-start(f32[352,256]{1,0:T(8,128)S(1)} %get-tuple-element.87), channel_id=1, source_target_pairs={{0,1},{1,0},{2,3},{3,2},{4,5},{5,4},{6,7},{7,6},{8,9},{9,8},{10,11... | collective-permute-start | bytes 1081352 | tf_op jit(solution)/shard_map/ppermute | solution.py:183
  156.9 2.6 %collective-permute-start.44 = (bf16[352,128]{1,0:T(8,128)(2,1)S(1)}, bf16[352,128]{1,0:T(8,128)(2,1)S(1)}, u32[]{:S(2)}, u32[]{:S(2)}) collective-permute-start(bf16[352,128]{1,0:T(8,128)(2,1)S(1)} %get-tuple-element.110), channel_id=1, source_target_pairs={{0,36},{1,49},{2,38},{3,51},{4,32},{5,53},{6,34},{7,55},{8,44},{9,... | collective-permute-start | bytes 270344 | tf_op jit(solution)/shard_map/ppermute | solution.py:180
  159.5 3.4 %collective-permute-start.45 = (bf16[352,128]{1,0:T(8,128)(2,1)S(1)}, bf16[352,128]{1,0:T(8,128)(2,1)S(1)}, u32[]{:S(2)}, u32[]{:S(2)}) collective-permute-start(bf16[352,128]{1,0:T(8,128)(2,1)S(1)} %get-tuple-element.110), channel_id=1, source_target_pairs={{0,38},{1,57},{2,32},{3,59},{4,34},{5,61},{6,36},{7,63},{8,46},{9,... | collective-permute-start | bytes 270344 | tf_op jit(solution)/shard_map/ppermute | solution.py:180
  162.9 2.4 %collective-permute-done.43 = bf16[352,128]{1,0:T(8,128)(2,1)S(1)} collective-permute-done((bf16[352,128]{1,0:T(8,128)(2,1)S(1)}, bf16[352,128]{1,0:T(8,128)(2,1)S(1)}, u32[]{:S(2)}, u32[]{:S(2)}) %collective-permute-start.43) | collective-permute-done | bytes 90144 | tf_op jit(solution)/shard_map/ppermute | solution.py:180
  171.9 4.1 %collective-permute-done.48.refs_1_ = bf16[4,352,128]{2,1,0:T(8,128)(2,1)S(1)} collective-permute-done((bf16[4,352,128]{2,1,0:T(8,128)(2,1)S(1)}, bf16[4,352,128]{2,1,0:T(8,128)(2,1)S(1)}, u32[]{:S(2)}, u32[]{:S(2)}) %collective-permute-start.48) | collective-permute-done | bytes 360480 | tf_op jit(solution)/shard_map/ppermute | solution.py:180
  176.0 3.1 %shard_map.80 = (f32[352,128]{1,0:T(8,128)S(1)}, f32[352,256]{1,0:T(8,128)S(1)}) custom-call(bf16[4,352,128]{2,1,0:T(8,128)(2,1)S(1)} %pad_maximum_fusion.5.refs_0_, bf16[4,352,128]{2,1,0:T(8,128)(2,1)S(1)} %collective-permute-done.48.refs_1_, bf16[8,2048,256]{2,1,0:T(8,128)(2,1)S(1)} %shard_map.69.refs_2_, f32[352,8]{1,0:T(8,128)S(1)} %get-tuple-element.88.refs_3_, ...), custom_call_target="tpu_custom_call" | custom-call | tf_op jit(solution)/shard_map/pallas_call | solution.py:146
  (119 shorter events, 87.9 us)
Async XLA Ops:
  6.6 19.4 %collective-permute-start.7 = (bf16[8,2048,128]{2,1,0:T(8,128)(2,1)}, bf16[8,2048,128]{2,1,0:T(8,128)(2,1)S(1)}, u32[]{:S(2)}, u32[]{:S(2)}) collective-permute-start(bf16[8,2048,128]{2,1,0:T(8,128)(2,1)} %shard_map.68), channel_id=1, source_target_pairs={{0,1},{1,0},{2,3},{3,2},{4,5},{5,4},{6,7},{7,6},{8,9},{9,8},{10,11... | collective-permute-start | bytes 12582920 | tf_op jit(solution)/shard_map/ppermute | solution.py:183
  6.8 8.5 %collective-permute-start.1 = (bf16[352,128]{1,0:T(8,128)(2,1)S(1)}, bf16[352,128]{1,0:T(8,128)(2,1)S(1)}, u32[]{:S(2)}, u32[]{:S(2)}) collective-permute-start(bf16[352,128]{1,0:T(8,128)(2,1)S(1)} %slice.96), channel_id=1, source_target_pairs={{0,32},{1,33},{2,34},{3,35},{4,36},{5,37},{6,38},{7,39},{8,40},{9,... | collective-permute-start | bytes 270344 | tf_op jit(solution)/shard_map/ppermute | solution.py:180
  8.2 8.8 %collective-permute-start.2 = (bf16[352,128]{1,0:T(8,128)(2,1)S(1)}, bf16[352,128]{1,0:T(8,128)(2,1)S(1)}, u32[]{:S(2)}, u32[]{:S(2)}) collective-permute-start(bf16[352,128]{1,0:T(8,128)(2,1)S(1)} %slice.96), channel_id=1, source_target_pairs={{0,34},{1,41},{2,36},{3,43},{4,38},{5,45},{6,32},{7,47},{8,42},{9,... | collective-permute-start | bytes 270344 | tf_op jit(solution)/shard_map/ppermute | solution.py:180
  10.7 8.4 %collective-permute-start.3 = (bf16[352,128]{1,0:T(8,128)(2,1)S(1)}, bf16[352,128]{1,0:T(8,128)(2,1)S(1)}, u32[]{:S(2)}, u32[]{:S(2)}) collective-permute-start(bf16[352,128]{1,0:T(8,128)(2,1)S(1)} %slice.96), channel_id=1, source_target_pairs={{0,36},{1,49},{2,38},{3,51},{4,32},{5,53},{6,34},{7,55},{8,44},{9,... | collective-permute-start | bytes 270344 | tf_op jit(solution)/shard_map/ppermute | solution.py:180
  21.4 8.2 %collective-permute-start.8 = (bf16[4,352,128]{2,1,0:T(8,128)(2,1)S(1)}, bf16[4,352,128]{2,1,0:T(8,128)(2,1)S(1)}, u32[]{:S(2)}, u32[]{:S(2)}) collective-permute-start(bf16[4,352,128]{2,1,0:T(8,128)(2,1)S(1)} %pad_maximum_fusion.refs_0_), channel_id=1, source_target_pairs={{0,16},{1,5},{2,18},{3,7},{4,20},{5,1},{6,22},{7,3},{8,24},{9,13},... | collective-permute-start | bytes 1081352 | tf_op jit(solution)/shard_map/ppermute | solution.py:180
  23.4 10.1 %collective-permute-start.5 = (bf16[4,352,128]{2,1,0:T(8,128)(2,1)S(1)}, bf16[4,352,128]{2,1,0:T(8,128)(2,1)S(1)}, u32[]{:S(2)}, u32[]{:S(2)}) collective-permute-start(bf16[4,352,128]{2,1,0:T(8,128)(2,1)S(1)} %pad_maximum_fusion.refs_0_), channel_id=1, source_target_pairs={{0,8},{1,3},{2,10},{3,5},{4,12},{5,7},{6,14},{7,1},{8,16},{9,11},{... | collective-permute-start | bytes 1081352 | tf_op jit(solution)/shard_map/ppermute | solution.py:180
  24.1 9.3 %collective-permute-start.6 = (bf16[4,352,128]{2,1,0:T(8,128)(2,1)S(1)}, bf16[4,352,128]{2,1,0:T(8,128)(2,1)S(1)}, u32[]{:S(2)}, u32[]{:S(2)}) collective-permute-start(bf16[4,352,128]{2,1,0:T(8,128)(2,1)S(1)} %pad_maximum_fusion.refs_0_), channel_id=1, source_target_pairs={{0,24},{1,7},{2,26},{3,1},{4,28},{5,3},{6,30},{7,5},{8,0},{9,15},{... | collective-permute-start | bytes 1081352 | tf_op jit(solution)/shard_map/ppermute | solution.py:180
  39.7 9.5 %collective-permute-start.13 = (bf16[352,128]{1,0:T(8,128)(2,1)S(1)}, bf16[352,128]{1,0:T(8,128)(2,1)S(1)}, u32[]{:S(2)}, u32[]{:S(2)}) collective-permute-start(bf16[352,128]{1,0:T(8,128)(2,1)S(1)} %get-tuple-element.122), channel_id=1, source_target_pairs={{0,38},{1,57},{2,32},{3,59},{4,34},{5,61},{6,36},{7,63},{8,46},{9,... | collective-permute-start | bytes 270344 | tf_op jit(solution)/shard_map/ppermute | solution.py:180
  41.9 8.3 %collective-permute-start.10 = (bf16[352,128]{1,0:T(8,128)(2,1)S(1)}, bf16[352,128]{1,0:T(8,128)(2,1)S(1)}, u32[]{:S(2)}, u32[]{:S(2)}) collective-permute-start(bf16[352,128]{1,0:T(8,128)(2,1)S(1)} %get-tuple-element.122), channel_id=1, source_target_pairs={{0,32},{1,33},{2,34},{3,35},{4,36},{5,37},{6,38},{7,39},{8,40},{9,... | collective-permute-start | bytes 270344 | tf_op jit(solution)/shard_map/ppermute | solution.py:180
  43.1 9.1 %collective-permute-start.11 = (bf16[352,128]{1,0:T(8,128)(2,1)S(1)}, bf16[352,128]{1,0:T(8,128)(2,1)S(1)}, u32[]{:S(2)}, u32[]{:S(2)}) collective-permute-start(bf16[352,128]{1,0:T(8,128)(2,1)S(1)} %get-tuple-element.122), channel_id=1, source_target_pairs={{0,34},{1,41},{2,36},{3,43},{4,38},{5,45},{6,32},{7,47},{8,42},{9,... | collective-permute-start | bytes 270344 | tf_op jit(solution)/shard_map/ppermute | solution.py:180
  52.3 8.2 %collective-permute-start.16 = (bf16[4,352,128]{2,1,0:T(8,128)(2,1)S(1)}, bf16[4,352,128]{2,1,0:T(8,128)(2,1)S(1)}, u32[]{:S(2)}, u32[]{:S(2)}) collective-permute-start(bf16[4,352,128]{2,1,0:T(8,128)(2,1)S(1)} %pad_maximum_fusion.1.refs_0_), channel_id=1, source_target_pairs={{0,16},{1,5},{2,18},{3,7},{4,20},{5,1},{6,22},{7,3},{8,24},{9,13},... | collective-permute-start | bytes 1081352 | tf_op jit(solution)/shard_map/ppermute | solution.py:180
  52.8 11.5 %collective-permute-start.14 = (bf16[4,352,128]{2,1,0:T(8,128)(2,1)S(1)}, bf16[4,352,128]{2,1,0:T(8,128)(2,1)S(1)}, u32[]{:S(2)}, u32[]{:S(2)}) collective-permute-start(bf16[4,352,128]{2,1,0:T(8,128)(2,1)S(1)} %pad_maximum_fusion.1.refs_0_), channel_id=1, source_target_pairs={{0,8},{1,3},{2,10},{3,5},{4,12},{5,7},{6,14},{7,1},{8,16},{9,11},{... | collective-permute-start | bytes 1081352 | tf_op jit(solution)/shard_map/ppermute | solution.py:180
  55.5 9.0 %collective-permute-start.15 = (bf16[4,352,128]{2,1,0:T(8,128)(2,1)S(1)}, bf16[4,352,128]{2,1,0:T(8,128)(2,1)S(1)}, u32[]{:S(2)}, u32[]{:S(2)}) collective-permute-start(bf16[4,352,128]{2,1,0:T(8,128)(2,1)S(1)} %pad_maximum_fusion.1.refs_0_), channel_id=1, source_target_pairs={{0,24},{1,7},{2,26},{3,1},{4,28},{5,3},{6,30},{7,5},{8,0},{9,15},{... | collective-permute-start | bytes 1081352 | tf_op jit(solution)/shard_map/ppermute | solution.py:180
  70.1 8.8 %collective-permute-start.19 = (bf16[352,128]{1,0:T(8,128)(2,1)S(1)}, bf16[352,128]{1,0:T(8,128)(2,1)S(1)}, u32[]{:S(2)}, u32[]{:S(2)}) collective-permute-start(bf16[352,128]{1,0:T(8,128)(2,1)S(1)} %get-tuple-element.119), channel_id=1, source_target_pairs={{0,34},{1,41},{2,36},{3,43},{4,38},{5,45},{6,32},{7,47},{8,42},{9,... | collective-permute-start | bytes 270344 | tf_op jit(solution)/shard_map/ppermute | solution.py:180
  70.3 10.3 %collective-permute-start.20 = (bf16[352,128]{1,0:T(8,128)(2,1)S(1)}, bf16[352,128]{1,0:T(8,128)(2,1)S(1)}, u32[]{:S(2)}, u32[]{:S(2)}) collective-permute-start(bf16[352,128]{1,0:T(8,128)(2,1)S(1)} %get-tuple-element.119), channel_id=1, source_target_pairs={{0,36},{1,49},{2,38},{3,51},{4,32},{5,53},{6,34},{7,55},{8,44},{9,... | collective-permute-start | bytes 270344 | tf_op jit(solution)/shard_map/ppermute | solution.py:180
  73.0 8.2 %collective-permute-start.21 = (bf16[352,128]{1,0:T(8,128)(2,1)S(1)}, bf16[352,128]{1,0:T(8,128)(2,1)S(1)}, u32[]{:S(2)}, u32[]{:S(2)}) collective-permute-start(bf16[352,128]{1,0:T(8,128)(2,1)S(1)} %get-tuple-element.119), channel_id=1, source_target_pairs={{0,38},{1,57},{2,32},{3,59},{4,34},{5,61},{6,36},{7,63},{8,46},{9,... | collective-permute-start | bytes 270344 | tf_op jit(solution)/shard_map/ppermute | solution.py:180
  81.3 8.2 %collective-permute-start.24 = (bf16[4,352,128]{2,1,0:T(8,128)(2,1)S(1)}, bf16[4,352,128]{2,1,0:T(8,128)(2,1)S(1)}, u32[]{:S(2)}, u32[]{:S(2)}) collective-permute-start(bf16[4,352,128]{2,1,0:T(8,128)(2,1)S(1)} %pad_maximum_fusion.2.refs_0_), channel_id=1, source_target_pairs={{0,16},{1,5},{2,18},{3,7},{4,20},{5,1},{6,22},{7,3},{8,24},{9,13},... | collective-permute-start | bytes 1081352 | tf_op jit(solution)/shard_map/ppermute | solution.py:180
  82.6 10.7 %collective-permute-start.22 = (bf16[4,352,128]{2,1,0:T(8,128)(2,1)S(1)}, bf16[4,352,128]{2,1,0:T(8,128)(2,1)S(1)}, u32[]{:S(2)}, u32[]{:S(2)}) collective-permute-start(bf16[4,352,128]{2,1,0:T(8,128)(2,1)S(1)} %pad_maximum_fusion.2.refs_0_), channel_id=1, source_target_pairs={{0,8},{1,3},{2,10},{3,5},{4,12},{5,7},{6,14},{7,1},{8,16},{9,11},{... | collective-permute-start | bytes 1081352 | tf_op jit(solution)/shard_map/ppermute | solution.py:180
  82.6 10.7 %collective-permute-start.23 = (bf16[4,352,128]{2,1,0:T(8,128)(2,1)S(1)}, bf16[4,352,128]{2,1,0:T(8,128)(2,1)S(1)}, u32[]{:S(2)}, u32[]{:S(2)}) collective-permute-start(bf16[4,352,128]{2,1,0:T(8,128)(2,1)S(1)} %pad_maximum_fusion.2.refs_0_), channel_id=1, source_target_pairs={{0,24},{1,7},{2,26},{3,1},{4,28},{5,3},{6,30},{7,5},{8,0},{9,15},{... | collective-permute-start | bytes 1081352 | tf_op jit(solution)/shard_map/ppermute | solution.py:180
  98.9 8.6 %collective-permute-start.28 = (bf16[352,128]{1,0:T(8,128)(2,1)S(1)}, bf16[352,128]{1,0:T(8,128)(2,1)S(1)}, u32[]{:S(2)}, u32[]{:S(2)}) collective-permute-start(bf16[352,128]{1,0:T(8,128)(2,1)S(1)} %get-tuple-element.116), channel_id=1, source_target_pairs={{0,36},{1,49},{2,38},{3,51},{4,32},{5,53},{6,34},{7,55},{8,44},{9,... | collective-permute-start | bytes 270344 | tf_op jit(solution)/shard_map/ppermute | solution.py:180
  108.9 8.2 %collective-permute-start.32 = (bf16[4,352,128]{2,1,0:T(8,128)(2,1)S(1)}, bf16[4,352,128]{2,1,0:T(8,128)(2,1)S(1)}, u32[]{:S(2)}, u32[]{:S(2)}) collective-permute-start(bf16[4,352,128]{2,1,0:T(8,128)(2,1)S(1)} %pad_maximum_fusion.3.refs_0_), channel_id=1, source_target_pairs={{0,16},{1,5},{2,18},{3,7},{4,20},{5,1},{6,22},{7,3},{8,24},{9,13},... | collective-permute-start | bytes 1081352 | tf_op jit(solution)/shard_map/ppermute | solution.py:180
  111.1 9.8 %collective-permute-start.30 = (bf16[4,352,128]{2,1,0:T(8,128)(2,1)S(1)}, bf16[4,352,128]{2,1,0:T(8,128)(2,1)S(1)}, u32[]{:S(2)}, u32[]{:S(2)}) collective-permute-start(bf16[4,352,128]{2,1,0:T(8,128)(2,1)S(1)} %pad_maximum_fusion.3.refs_0_), channel_id=1, source_target_pairs={{0,8},{1,3},{2,10},{3,5},{4,12},{5,7},{6,14},{7,1},{8,16},{9,11},{... | collective-permute-start | bytes 1081352 | tf_op jit(solution)/shard_map/ppermute | solution.py:180
  112.6 9.0 %collective-permute-start.31 = (bf16[4,352,128]{2,1,0:T(8,128)(2,1)S(1)}, bf16[4,352,128]{2,1,0:T(8,128)(2,1)S(1)}, u32[]{:S(2)}, u32[]{:S(2)}) collective-permute-start(bf16[4,352,128]{2,1,0:T(8,128)(2,1)S(1)} %pad_maximum_fusion.3.refs_0_), channel_id=1, source_target_pairs={{0,24},{1,7},{2,26},{3,1},{4,28},{5,3},{6,30},{7,5},{8,0},{9,15},{... | collective-permute-start | bytes 1081352 | tf_op jit(solution)/shard_map/ppermute | solution.py:180
  128.1 8.6 %collective-permute-start.36 = (bf16[352,128]{1,0:T(8,128)(2,1)S(1)}, bf16[352,128]{1,0:T(8,128)(2,1)S(1)}, u32[]{:S(2)}, u32[]{:S(2)}) collective-permute-start(bf16[352,128]{1,0:T(8,128)(2,1)S(1)} %get-tuple-element.113), channel_id=1, source_target_pairs={{0,36},{1,49},{2,38},{3,51},{4,32},{5,53},{6,34},{7,55},{8,44},{9,... | collective-permute-start | bytes 270344 | tf_op jit(solution)/shard_map/ppermute | solution.py:180
  137.3 8.8 %collective-permute-start.40 = (bf16[4,352,128]{2,1,0:T(8,128)(2,1)S(1)}, bf16[4,352,128]{2,1,0:T(8,128)(2,1)S(1)}, u32[]{:S(2)}, u32[]{:S(2)}) collective-permute-start(bf16[4,352,128]{2,1,0:T(8,128)(2,1)S(1)} %pad_maximum_fusion.4.refs_0_), channel_id=1, source_target_pairs={{0,16},{1,5},{2,18},{3,7},{4,20},{5,1},{6,22},{7,3},{8,24},{9,13},... | collective-permute-start | bytes 1081352 | tf_op jit(solution)/shard_map/ppermute | solution.py:180
  141.1 9.0 %collective-permute-start.38 = (bf16[4,352,128]{2,1,0:T(8,128)(2,1)S(1)}, bf16[4,352,128]{2,1,0:T(8,128)(2,1)S(1)}, u32[]{:S(2)}, u32[]{:S(2)}) collective-permute-start(bf16[4,352,128]{2,1,0:T(8,128)(2,1)S(1)} %pad_maximum_fusion.4.refs_0_), channel_id=1, source_target_pairs={{0,8},{1,3},{2,10},{3,5},{4,12},{5,7},{6,14},{7,1},{8,16},{9,11},{... | collective-permute-start | bytes 1081352 | tf_op jit(solution)/shard_map/ppermute | solution.py:180
  141.1 9.0 %collective-permute-start.39 = (bf16[4,352,128]{2,1,0:T(8,128)(2,1)S(1)}, bf16[4,352,128]{2,1,0:T(8,128)(2,1)S(1)}, u32[]{:S(2)}, u32[]{:S(2)}) collective-permute-start(bf16[4,352,128]{2,1,0:T(8,128)(2,1)S(1)} %pad_maximum_fusion.4.refs_0_), channel_id=1, source_target_pairs={{0,24},{1,7},{2,26},{3,1},{4,28},{5,3},{6,30},{7,5},{8,0},{9,15},{... | collective-permute-start | bytes 1081352 | tf_op jit(solution)/shard_map/ppermute | solution.py:180
  156.6 8.7 %collective-permute-start.43 = (bf16[352,128]{1,0:T(8,128)(2,1)S(1)}, bf16[352,128]{1,0:T(8,128)(2,1)S(1)}, u32[]{:S(2)}, u32[]{:S(2)}) collective-permute-start(bf16[352,128]{1,0:T(8,128)(2,1)S(1)} %get-tuple-element.110), channel_id=1, source_target_pairs={{0,34},{1,41},{2,36},{3,43},{4,38},{5,45},{6,32},{7,47},{8,42},{9,... | collective-permute-start | bytes 270344 | tf_op jit(solution)/shard_map/ppermute | solution.py:180
  156.9 10.2 %collective-permute-start.44 = (bf16[352,128]{1,0:T(8,128)(2,1)S(1)}, bf16[352,128]{1,0:T(8,128)(2,1)S(1)}, u32[]{:S(2)}, u32[]{:S(2)}) collective-permute-start(bf16[352,128]{1,0:T(8,128)(2,1)S(1)} %get-tuple-element.110), channel_id=1, source_target_pairs={{0,36},{1,49},{2,38},{3,51},{4,32},{5,53},{6,34},{7,55},{8,44},{9,... | collective-permute-start | bytes 270344 | tf_op jit(solution)/shard_map/ppermute | solution.py:180
  159.5 8.2 %collective-permute-start.45 = (bf16[352,128]{1,0:T(8,128)(2,1)S(1)}, bf16[352,128]{1,0:T(8,128)(2,1)S(1)}, u32[]{:S(2)}, u32[]{:S(2)}) collective-permute-start(bf16[352,128]{1,0:T(8,128)(2,1)S(1)} %get-tuple-element.110), channel_id=1, source_target_pairs={{0,38},{1,57},{2,32},{3,59},{4,34},{5,61},{6,36},{7,63},{8,46},{9,... | collective-permute-start | bytes 270344 | tf_op jit(solution)/shard_map/ppermute | solution.py:180
  169.1 10.7 %collective-permute-start.46 = (bf16[4,352,128]{2,1,0:T(8,128)(2,1)S(1)}, bf16[4,352,128]{2,1,0:T(8,128)(2,1)S(1)}, u32[]{:S(2)}, u32[]{:S(2)}) collective-permute-start(bf16[4,352,128]{2,1,0:T(8,128)(2,1)S(1)} %pad_maximum_fusion.5.refs_0_), channel_id=1, source_target_pairs={{0,8},{1,3},{2,10},{3,5},{4,12},{5,7},{6,14},{7,1},{8,16},{9,11},{... | collective-permute-start | bytes 1081352 | tf_op jit(solution)/shard_map/ppermute | solution.py:180
  170.0 9.8 %collective-permute-start.47 = (bf16[4,352,128]{2,1,0:T(8,128)(2,1)S(1)}, bf16[4,352,128]{2,1,0:T(8,128)(2,1)S(1)}, u32[]{:S(2)}, u32[]{:S(2)}) collective-permute-start(bf16[4,352,128]{2,1,0:T(8,128)(2,1)S(1)} %pad_maximum_fusion.5.refs_0_), channel_id=1, source_target_pairs={{0,24},{1,7},{2,26},{3,1},{4,28},{5,3},{6,30},{7,5},{8,0},{9,15},{... | collective-permute-start | bytes 1081352 | tf_op jit(solution)/shard_map/ppermute | solution.py:180
  (22 other events, 125.5 us)
